TPU v7x, 256 devices: a whole 4x4x8 slice. The times are simulated.
256 devices in a mesh: dp: 128 (over z, y, x_lo, core), tensor: 2 (over x_hi).
Axes of the slice: x: 4 (x_hi: 2, x_lo: 2; x = x_hi * 2 + x_lo), y: 4, z: 8, core: 2. Of those that a mesh axis runs over, the one named last changes fastest.
Arguments:
- source_frames: bfloat16 [32768, 1536], P(('dp', 'tensor')), may hold values from -24 to 24
- routes: int32 [32768, 1], P(('dp', 'tensor')), may hold values from 0 to 127; in each aligned block of 128 rows (0 to 127, 128 to 255, ...) at most 2 rows name the same one
- live_frames: int32 [256], P(('dp', 'tensor')), may hold values from 32 to 128
- norm_gain: float32 [1536], replicated, may hold values from 0.1 to 1.9
- weight_in: bfloat16 [1536, 3072], P(None, 'tensor'), may hold values from -0.15625 to 0.15625
- weight_out: bfloat16 [3072, 1536], P('tensor'), may hold values from -0.109375 to 0.109375
- cotangent: bfloat16 [65536, 1536], P(('dp', 'tensor')), may hold values from -24 to 24
Outputs:
- mixed: bfloat16 [65536, 1536], P(('dp', 'tensor'))
- grad_source: bfloat16 [32768, 1536], P(('dp', 'tensor'))
- grad_out: float32 [3072, 1536], P('tensor', 'dp')
Inputs may be any that keep to these rules, and one draw needn't show every extreme that they name: `routes`: among the slots of one device, no destination index is named by more than 2 slots, a bound that some block reaches.
All inputs are finite; a program needn't handle non-finite values.
Results may differ from a plain program's by a relative error of at most 0.008.
Values may be sent and summed in bfloat16 or wider, within the bound.
A program may use at most 128 MiB of HBM per device.

v0:
```python
import jax
import jax.numpy as jnp
from jax import lax
from jax.sharding import PartitionSpec as P

epsilon = 1e-05


def local(source_frames, routes, live_frames, norm_gain, weight_in, weight_out, cotangent):
    frame_count = source_frames.shape[0]
    width = source_frames.shape[1]
    dest_rows = cotangent.shape[0]
    dest_count = lax.axis_size("dp")
    capacity = dest_rows // dest_count
    target = routes[:, 0]
    one_hot = (
        target[:, None] == lax.broadcasted_iota(jnp.int32, (frame_count, dest_count), 1)
    ).astype(jnp.int32)
    before = jnp.cumsum(one_hot, axis=0) - one_hot
    send_slot = target * capacity + jnp.sum(before * one_hot, axis=1)
    alive_mask = (lax.broadcasted_iota(jnp.int32, (frame_count, 1), 0) < live_frames[0]).astype(
        jnp.bfloat16
    )
    outgoing = (
        jnp.zeros((dest_rows, width), jnp.bfloat16).at[send_slot].set(source_frames * alive_mask)
    )
    present_flags = jnp.zeros((dest_rows,), jnp.bfloat16).at[send_slot].set(alive_mask[:, 0])
    arrived, present = (
        lax.all_to_all(outgoing, "dp", split_axis=0, concat_axis=0, tiled=True),
        lax.all_to_all(present_flags, "dp", split_axis=0, concat_axis=0, tiled=True),
    )
    frames_f = arrived.astype(jnp.float32)
    row_mean = jnp.mean(frames_f, axis=1, keepdims=True)
    centred = frames_f - row_mean
    row_var = jnp.mean(centred * centred, axis=1, keepdims=True)
    inv_std = lax.rsqrt(row_var + epsilon)
    normed = centred * inv_std
    scaled = (normed * norm_gain).astype(jnp.bfloat16)
    scaled_all = lax.all_gather(scaled, "tensor", axis=0, tiled=True)
    hidden = jnp.dot(scaled_all, weight_in, preferred_element_type=jnp.float32)
    sigmoid_gate = jax.nn.sigmoid(hidden)
    activated = (hidden * sigmoid_gate).astype(jnp.bfloat16)
    piece = activated
    mixed_sum = lax.psum_scatter(
        jnp.dot(piece, weight_out, preferred_element_type=jnp.float32).astype(jnp.bfloat16),
        "tensor",
        scatter_dimension=0,
        tiled=True,
    ).astype(jnp.float32)
    output_rows = (frames_f + 0.5 * mixed_sum).astype(jnp.bfloat16)
    grad_rows = cotangent * present[:, None]
    grad_all = lax.all_gather(grad_rows, "tensor", axis=0, tiled=True)
    grad_out = 0.5 * jnp.dot(activated.T, grad_all, preferred_element_type=jnp.float32)
    grad_act = 0.5 * jnp.dot(grad_all, weight_out.T, preferred_element_type=jnp.float32)
    grad_hidden = (grad_act * sigmoid_gate * (1.0 + hidden * (1.0 - sigmoid_gate))).astype(
        jnp.bfloat16
    )
    piece = grad_hidden
    grad_scaled = lax.psum_scatter(
        jnp.dot(piece, weight_in.T, preferred_element_type=jnp.float32).astype(jnp.bfloat16),
        "tensor",
        scatter_dimension=0,
        tiled=True,
    ).astype(jnp.float32)
    grad_normed = grad_scaled * norm_gain
    first_mean = jnp.mean(grad_normed, axis=1, keepdims=True)
    second_mean = jnp.mean(grad_normed * normed, axis=1, keepdims=True)
    grad_frames = (
        grad_rows.astype(jnp.float32) + inv_std * (grad_normed - first_mean - normed * second_mean)
    ).astype(jnp.bfloat16)
    returned = lax.all_to_all(grad_frames, "dp", split_axis=0, concat_axis=0, tiled=True)
    grad_source = returned[send_slot] * alive_mask
    grad_out_part = lax.psum_scatter(grad_out, "dp", scatter_dimension=1, tiled=True)
    return (output_rows, grad_source, grad_out_part)


def solution(mesh):
    return jax.shard_map(
        local,
        mesh=mesh,
        in_specs=(
            P(("dp", "tensor"), None),
            P(("dp", "tensor"), None),
            P(("dp", "tensor")),
            P(),
            P(None, "tensor"),
            P("tensor", None),
            P(("dp", "tensor"), None),
        ),
        out_specs=(P(("dp", "tensor"), None), P(("dp", "tensor"), None), P("tensor", "dp")),
        check_vma=False,
    )
```

profile of v0, /device:TPU:1, one launch (start us, length us, event | category | flops | bytes accessed | tf_op | source)
XLA Modules:
  0.0 699.4 jit_solution(16514090188321745831)
XLA Ops:
  12.6 38.6 %all_to_all.31 = bf16[128,2,1536]{2,1,0:T(2,128)(2,1)S(1)} all-to-all(bf16[128,2,1536]{2,1,0:T(2,128)(2,1)S(1)} %all_to_all.20), channel_id=1, replica_groups=mesh['dp'=128,'tensor'=2] {'dp'}, dimensions={0} | all-to-all | bytes 1572864 | tf_op jit(solution)/shard_map/all_to_all | solution.py:29
  56.4 17.1 %all_to_all.32 = bf16[128,2,1]{1,2,0:T(2,128)(2,1)S(1)} all-to-all(bf16[128,2,1]{1,2,0:T(2,128)(2,1)S(1)} %all_to_all.27), channel_id=1, replica_groups=mesh['dp'=128,'tensor'=2] {'dp'}, dimensions={0} | all-to-all | bytes 1024 | tf_op jit(solution)/shard_map/all_to_all | solution.py:30
  75.1 10.5 %all-gather.3.cloned.1.call-done = bf16[512,1536]{1,0:T(8,128)(2,1)} async-done(((bf16[256,1536]{1,0:T(8,128)(2,1)}), bf16[512,1536]{1,0:T(8,128)(2,1)}) %all-gather.3.cloned.1.call-update) | async-done | bytes 1572880 | tf_op jit(solution)/shard_map/all_gather | solution.py:39
  85.6 7.1 %fusion.15 = f32[512,1536]{1,0:T(8,128)} fusion(bf16[512,1536]{1,0:T(8,128)(2,1)} %all-gather.3.cloned.1.call-done, bf16[1536,1536]{1,0:T(8,128)(2,1)} %param.11), kind=kOutput, calls=%fused_computation.44 | convolution fusion | flops 2415919104 | bytes 9437184 | tf_op jit(solution)/shard_map/dot_general | solution.py:40
  92.7 27.4 %all-gather.5.cloned.1.call-done = bf16[512,1536]{1,0:T(8,128)(2,1)} async-done(((bf16[256,1536]{1,0:T(8,128)(2,1)}), bf16[512,1536]{1,0:T(8,128)(2,1)}) %all-gather.5.cloned.1.call-update) | async-done | bytes 1572880 | tf_op jit(solution)/shard_map/all_gather | solution.py:52
  120.1 11.6 %convolution_convert_fusion = bf16[512,1536]{1,0:T(8,128)(2,1)} fusion(bf16[1536,1536]{1,0:T(8,128)(2,1)} %param.11, f32[512,1536]{1,0:T(8,128)} %fusion.15, bf16[512,1536]{1,0:T(8,128)(2,1)} %all-gather.5.cloned.1.call-done, bf16[1536,1536]{1,0:T(8,128)(2,1)} %param.12), kind=kOutput, calls=%fused_computation.10 | convolution fusion | flops 4840488960 | bytes 15728640 | tf_op jit(solution)/shard_map/dot_general | solution.py:60
  131.7 7.1 %convolution_convert_fusion.1 = bf16[512,1536]{1,0:T(8,128)(2,1)} fusion(bf16[1536,1536]{1,0:T(8,128)(2,1)} %param.12, f32[512,1536]{1,0:T(8,128)} %fusion.15), kind=kOutput, calls=%fused_computation.11 | convolution fusion | flops 2420637696 | bytes 9437184 | tf_op jit(solution)/shard_map/dot_general | solution.py:45
  138.8 8.7 %convolution_multiply_fusion = f32[1536,1536]{0,1:T(8,128)} fusion(bf16[512,1536]{1,0:T(8,128)(2,1)} %all-gather.5.cloned.1.call-done, f32[512,1536]{1,0:T(8,128)} %fusion.15), kind=kOutput, calls=%fused_computation.3 | convolution fusion | flops 2422210560 | bytes 14155776 | tf_op jit(solution)/shard_map/dot_general | solution.py:53
  147.5 16.4 %reduce-scatter.7.cloned.1.call-done = bf16[256,1536]{1,0:T(8,128)(2,1)} async-done(((bf16[512,1536]{1,0:T(8,128)(2,1)}), bf16[256,1536]{1,0:T(8,128)(2,1)}) %reduce-scatter.7.cloned.1.call-update) | async-done | bytes 786448 | tf_op jit(solution)/shard_map/reduce_scatter | solution.py:59
  165.6 33.1 %reduce-scatter.5.cloned.1.call-done = bf16[256,1536]{1,0:T(8,128)(2,1)} async-done(((bf16[512,1536]{1,0:T(8,128)(2,1)}), bf16[256,1536]{1,0:T(8,128)(2,1)}) %reduce-scatter.5.cloned.1.call-update) | async-done | bytes 786448 | tf_op jit(solution)/shard_map/reduce_scatter | solution.py:44
  202.7 11.9 %all-to-all-start.2 = ((bf16[128,2,1536]{2,1,0:T(2,128)(2,1)}), bf16[128,2,1536]{2,1,0:T(2,128)(2,1)}, u32[]{:S(2)}, u32[]{:S(2)}) async-start(bf16[128,2,1536]{2,1,0:T(2,128)(2,1)} %all_to_all.24), calls=%async_computation.4 | async-start | bytes 1572864 | tf_op jit(solution)/shard_map/all_to_all | solution.py:71
  214.6 334.2 %fusion = f32[1536,16]{0,1:T(8,128)S(1)} fusion(f32[1536,1536]{0,1:T(8,128)} %convolution_multiply_fusion), kind=kCustom, calls=%all-reduce-scatter | all-reduce-scatter fusion | flops 3145729 | bytes 9536512
  550.2 9.4 %collective-permute-start.31 = (f32[1536,12]{0,1:T(8,128)S(1)}, f32[1536,12]{0,1:T(8,128)S(1)}, u32[]{:S(2)}, u32[]{:S(2)}) collective-permute-start(f32[1536,12]{0,1:T(8,128)S(1)} %slice.2), channel_id=1, source_target_pairs={{0,64},{2,66},{4,68},{6,70},{8,72},{10,74},{12,76},{14,78},{16,80}... | collective-permute-start | bytes 221192
  568.8 6.8 collective-permute-start.22
  575.7 7.0 collective-permute-start.21
  582.7 3.4 collective-permute-start.20
  592.7 10.5 %collective-permute-start.15 = (f32[1536,16]{0,1:T(8,128)S(1)}, f32[1536,16]{0,1:T(8,128)S(1)}, u32[]{:S(2)}, u32[]{:S(2)}) collective-permute-start(f32[1536,16]{0,1:T(8,128)S(1)} %fusion), channel_id=1, source_target_pairs={{0,32},{2,34},{4,36},{6,38},{8,40},{10,42},{12,44},{14,46},{16,48}... | collective-permute-start | bytes 294920
  610.8 10.1 %collective-permute-start.10 = (f32[1536,16]{0,1:T(8,128)S(1)}, f32[1536,16]{0,1:T(8,128)S(1)}, u32[]{:S(2)}, u32[]{:S(2)}) collective-permute-start(f32[1536,16]{0,1:T(8,128)S(1)} %fusion), channel_id=1, source_target_pairs={{0,22},{2,24},{4,26},{6,28},{8,30},{10,32},{12,34},{14,36},{16,38}... | collective-permute-start | bytes 294920
  626.9 6.7 collective-permute-start.7
  635.5 3.8 collective-permute-start.5
  640.7 5.2 collective-permute-start.4
  647.2 3.4 collective-permute-start.2
  653.2 3.4 collective-permute-start
  658.2 30.0 %concatenate = f32[1536,524]{0,1:T(8,128)S(1)} concatenate(f32[1536,12]{0,1:T(8,128)S(1)} %collective-permute-done.31, f32[1536,16]{0,1:T(8,128)S(1)} %collective-permute-done.30, f32[1536,16]{0,1:T(8,128)} %copy-done.1, f32[1536,16]{0,1:T(8,128)} %copy-done.2, f32[1536,16]{0,1:T(8,128)} %copy-done.3, f32[1536,16]{0,1:T(8,128)} %copy-done.4, f32[1536,16]{0,1:T(8,128)} %copy-done.5, ...), dimensions={1} | concatenate | bytes 6438912
  (157 shorter events, 60.0 us)
Async XLA Ops:
  7.2 78.4 %all-gather.3.cloned.1.call-start = ((), (), s32[]{:S(2)}) async-start(), calls=%async_computation.5 | async-start | bytes 2359296 | tf_op jit(solution)/shard_map/all_gather | solution.py:39
  54.8 65.3 %all-gather.5.cloned.1.call-start = ((), (), s32[]{:S(2)}) async-start(), calls=%async_computation.7 | async-start | bytes 2359296 | tf_op jit(solution)/shard_map/all_gather | solution.py:52
  74.9 89.1 %reduce-scatter.7.cloned.1.call-start = ((), (), s32[]{:S(2)}) async-start(), calls=%async_computation.8 | async-start | bytes 2359296 | tf_op jit(solution)/shard_map/reduce_scatter | solution.py:59
  131.7 67.0 %reduce-scatter.5.cloned.1.call-start = ((), (), s32[]{:S(2)}) async-start(), calls=%async_computation.6 | async-start | bytes 2359296 | tf_op jit(solution)/shard_map/reduce_scatter | solution.py:44
  202.7 486.1 %all-to-all-start.2 = ((bf16[128,2,1536]{2,1,0:T(2,128)(2,1)}), bf16[128,2,1536]{2,1,0:T(2,128)(2,1)}, u32[]{:S(2)}, u32[]{:S(2)}) async-start(bf16[128,2,1536]{2,1,0:T(2,128)(2,1)} %all_to_all.24), calls=%async_computation.4 | async-start | bytes 1572864 | tf_op jit(solution)/shard_map/all_to_all | solution.py:71
  564.8 17.8 %collective-permute-start.25 = (f32[1536,16]{0,1:T(8,128)S(1)}, f32[1536,16]{0,1:T(8,128)S(1)}, u32[]{:S(2)}, u32[]{:S(2)}) collective-permute-start(f32[1536,16]{0,1:T(8,128)S(1)} %fusion), channel_id=1, source_target_pairs={{0,52},{2,54},{4,56},{6,58},{8,60},{10,62},{12,64},{14,66},{16,68}... | collective-permute-start | bytes 294920
  566.1 20.0 %collective-permute-start.24 = (f32[1536,16]{0,1:T(8,128)S(1)}, f32[1536,16]{0,1:T(8,128)S(1)}, u32[]{:S(2)}, u32[]{:S(2)}) collective-permute-start(f32[1536,16]{0,1:T(8,128)S(1)} %fusion), channel_id=1, source_target_pairs={{0,50},{2,52},{4,54},{6,56},{8,58},{10,60},{12,62},{14,64},{16,66}... | collective-permute-start | bytes 294920
  567.5 20.0 %collective-permute-start.23 = (f32[1536,16]{0,1:T(8,128)S(1)}, f32[1536,16]{0,1:T(8,128)S(1)}, u32[]{:S(2)}, u32[]{:S(2)}) collective-permute-start(f32[1536,16]{0,1:T(8,128)S(1)} %fusion), channel_id=1, source_target_pairs={{0,48},{2,50},{4,52},{6,54},{8,56},{10,58},{12,60},{14,62},{16,64}... | collective-permute-start | bytes 294920
  568.8 20.0 %collective-permute-start.22 = (f32[1536,16]{0,1:T(8,128)S(1)}, f32[1536,16]{0,1:T(8,128)S(1)}, u32[]{:S(2)}, u32[]{:S(2)}) collective-permute-start(f32[1536,16]{0,1:T(8,128)S(1)} %fusion), channel_id=1, source_target_pairs={{0,46},{2,48},{4,50},{6,52},{8,54},{10,56},{12,58},{14,60},{16,62}... | collective-permute-start | bytes 294920
  586.1 17.1 %collective-permute-start.19 = (f32[1536,16]{0,1:T(8,128)S(1)}, f32[1536,16]{0,1:T(8,128)S(1)}, u32[]{:S(2)}, u32[]{:S(2)}) collective-permute-start(f32[1536,16]{0,1:T(8,128)S(1)} %fusion), channel_id=1, source_target_pairs={{0,40},{2,42},{4,44},{6,46},{8,48},{10,50},{12,52},{14,54},{16,56}... | collective-permute-start | bytes 294920
  587.4 17.8 %collective-permute-start.18 = (f32[1536,16]{0,1:T(8,128)S(1)}, f32[1536,16]{0,1:T(8,128)S(1)}, u32[]{:S(2)}, u32[]{:S(2)}) collective-permute-start(f32[1536,16]{0,1:T(8,128)S(1)} %fusion), channel_id=1, source_target_pairs={{0,38},{2,40},{4,42},{6,44},{8,46},{10,48},{12,50},{14,52},{16,54}... | collective-permute-start | bytes 294920
  588.8 18.8 %collective-permute-start.17 = (f32[1536,16]{0,1:T(8,128)S(1)}, f32[1536,16]{0,1:T(8,128)S(1)}, u32[]{:S(2)}, u32[]{:S(2)}) collective-permute-start(f32[1536,16]{0,1:T(8,128)S(1)} %fusion), channel_id=1, source_target_pairs={{0,36},{2,38},{4,40},{6,42},{8,44},{10,46},{12,48},{14,50},{16,52}... | collective-permute-start | bytes 294920
  590.8 18.7 %collective-permute-start.16 = (f32[1536,16]{0,1:T(8,128)S(1)}, f32[1536,16]{0,1:T(8,128)S(1)}, u32[]{:S(2)}, u32[]{:S(2)}) collective-permute-start(f32[1536,16]{0,1:T(8,128)S(1)} %fusion), channel_id=1, source_target_pairs={{0,34},{2,36},{4,38},{6,40},{8,42},{10,44},{12,46},{14,48},{16,50}... | collective-permute-start | bytes 294920
  592.7 18.0 %collective-permute-start.15 = (f32[1536,16]{0,1:T(8,128)S(1)}, f32[1536,16]{0,1:T(8,128)S(1)}, u32[]{:S(2)}, u32[]{:S(2)}) collective-permute-start(f32[1536,16]{0,1:T(8,128)S(1)} %fusion), channel_id=1, source_target_pairs={{0,32},{2,34},{4,36},{6,38},{8,40},{10,42},{12,44},{14,46},{16,48}... | collective-permute-start | bytes 294920
  603.2 17.7 %collective-permute-start.14 = (f32[1536,16]{0,1:T(8,128)S(1)}, f32[1536,16]{0,1:T(8,128)S(1)}, u32[]{:S(2)}, u32[]{:S(2)}) collective-permute-start(f32[1536,16]{0,1:T(8,128)S(1)} %fusion), channel_id=1, source_target_pairs={{0,30},{2,32},{4,34},{6,36},{8,38},{10,40},{12,42},{14,44},{16,46}... | collective-permute-start | bytes 294920
  605.3 18.5 %collective-permute-start.13 = (f32[1536,16]{0,1:T(8,128)S(1)}, f32[1536,16]{0,1:T(8,128)S(1)}, u32[]{:S(2)}, u32[]{:S(2)}) collective-permute-start(f32[1536,16]{0,1:T(8,128)S(1)} %fusion), channel_id=1, source_target_pairs={{0,28},{2,30},{4,32},{6,34},{8,36},{10,38},{12,40},{14,42},{16,44}... | collective-permute-start | bytes 294920
  607.6 19.3 %collective-permute-start.12 = (f32[1536,16]{0,1:T(8,128)S(1)}, f32[1536,16]{0,1:T(8,128)S(1)}, u32[]{:S(2)}, u32[]{:S(2)}) collective-permute-start(f32[1536,16]{0,1:T(8,128)S(1)} %fusion), channel_id=1, source_target_pairs={{0,26},{2,28},{4,30},{6,32},{8,34},{10,36},{12,38},{14,40},{16,42}... | collective-permute-start | bytes 294920
  609.4 24.1 %collective-permute-start.11 = (f32[1536,16]{0,1:T(8,128)S(1)}, f32[1536,16]{0,1:T(8,128)S(1)}, u32[]{:S(2)}, u32[]{:S(2)}) collective-permute-start(f32[1536,16]{0,1:T(8,128)S(1)} %fusion), channel_id=1, source_target_pairs={{0,24},{2,26},{4,28},{6,30},{8,32},{10,34},{12,36},{14,38},{16,40}... | collective-permute-start | bytes 294920
  610.8 24.7 %collective-permute-start.10 = (f32[1536,16]{0,1:T(8,128)S(1)}, f32[1536,16]{0,1:T(8,128)S(1)}, u32[]{:S(2)}, u32[]{:S(2)}) collective-permute-start(f32[1536,16]{0,1:T(8,128)S(1)} %fusion), channel_id=1, source_target_pairs={{0,22},{2,24},{4,26},{6,28},{8,30},{10,32},{12,34},{14,36},{16,38}... | collective-permute-start | bytes 294920
  620.9 19.7 %collective-permute-start.9 = (f32[1536,16]{0,1:T(8,128)S(1)}, f32[1536,16]{0,1:T(8,128)S(1)}, u32[]{:S(2)}, u32[]{:S(2)}) collective-permute-start(f32[1536,16]{0,1:T(8,128)S(1)} %fusion), channel_id=1, source_target_pairs={{0,20},{2,22},{4,24},{6,26},{8,28},{10,30},{12,32},{14,34},{16,36}... | collective-permute-start | bytes 294920
  623.8 22.0 %collective-permute-start.8 = (f32[1536,16]{0,1:T(8,128)S(1)}, f32[1536,16]{0,1:T(8,128)S(1)}, u32[]{:S(2)}, u32[]{:S(2)}) collective-permute-start(f32[1536,16]{0,1:T(8,128)S(1)} %fusion), channel_id=1, source_target_pairs={{0,18},{2,20},{4,22},{6,24},{8,26},{10,28},{12,30},{14,32},{16,34}... | collective-permute-start | bytes 294920
  626.9 20.3 %collective-permute-start.7 = (f32[1536,16]{0,1:T(8,128)S(1)}, f32[1536,16]{0,1:T(8,128)S(1)}, u32[]{:S(2)}, u32[]{:S(2)}) collective-permute-start(f32[1536,16]{0,1:T(8,128)S(1)} %fusion), channel_id=1, source_target_pairs={{0,16},{2,18},{4,20},{6,22},{8,24},{10,26},{12,28},{14,30},{16,32}... | collective-permute-start | bytes 294920
  633.6 17.0 %collective-permute-start.6 = (f32[1536,16]{0,1:T(8,128)S(1)}, f32[1536,16]{0,1:T(8,128)S(1)}, u32[]{:S(2)}, u32[]{:S(2)}) collective-permute-start(f32[1536,16]{0,1:T(8,128)S(1)} %fusion), channel_id=1, source_target_pairs={{0,14},{2,16},{4,18},{6,20},{8,22},{10,24},{12,26},{14,28},{16,30}... | collective-permute-start | bytes 294920
  635.5 17.7 %collective-permute-start.5 = (f32[1536,16]{0,1:T(8,128)S(1)}, f32[1536,16]{0,1:T(8,128)S(1)}, u32[]{:S(2)}, u32[]{:S(2)}) collective-permute-start(f32[1536,16]{0,1:T(8,128)S(1)} %fusion), channel_id=1, source_target_pairs={{0,12},{2,14},{4,16},{6,18},{8,20},{10,22},{12,24},{14,26},{16,28}... | collective-permute-start | bytes 294920
  (45 other events, 1427.4 us)
Sparse Core Ops, SparseCore 0:
  54.9 30.6 all-gather.2
  87.4 32.6 all-gather.4
  131.8 32.1 reduce-scatter.6
  166.5 32.1 reduce-scatter.4
where the time goes:
time: 703 us; the launch traced here: 699 us
  blocking collectives  390 us (55%)
  starting transfers between devices  118 us (17%)
  waiting for transfers between devices  87.7 us (12%)
  local copies, waits for them, and re-layouts  39.5 us (6%)
  matrix products  34.5 us (5%)
  between operations  16.1 us (2%)
  other arithmetic  14 us (2%)
    unnamed x1, blocking collectives  334 us
    unnamed x32, starting transfers between devices  105 us
    all_to_all x1, blocking collectives, local(): lax.all_to_all(outgoing, 'dp', split_axis=0, concat_axis=0, tiled=True)  38.6 us
    reduce_scatter x1, waiting for transfers between devices, local(): lax.psum_scatter(jnp.dot(piece, weight_out, preferred_element_type=jnp.fl...  33.1 us
    unnamed x68, local copies, waits for them, and re-layouts  32.7 us
    all_gather x1, waiting for transfers between devices, local(): grad_all = lax.all_gather(grad_rows, 'tensor', axis=0, tiled=True)  27.4 us
    all_to_all x1, blocking collectives, local(): lax.all_to_all(present_flags, 'dp', split_axis=0, concat_axis=0, tiled=True)  17.1 us
    reduce_scatter x1, waiting for transfers between devices, local(): lax.psum_scatter(jnp.dot(piece, weight_in.T, preferred_element_type=jnp.f...  16.4 us
  transfers between devices with their start and end apart: 37, of which 5 were waited for; matrix products, arithmetic and copies ran while one was open for 56% of the time, Pallas kernels for 0%

commit v1 on v0

v1 whole, which is shorter than its diff:
```python
import functools

import jax
import jax.numpy as jnp
from jax import lax
from jax.experimental import pallas as pl
from jax.experimental.pallas import tpu as pltpu
from jax.sharding import PartitionSpec as P

epsilon = 1e-05
ABSENT = 64.0
MESH = pl.DeviceIdType.MESH
GROUP = 16


def on_dp(index):
    return {"dp": index}


def remote(src, dst, send_sem, recv_sem, index):
    return pltpu.make_async_remote_copy(
        src_ref=src,
        dst_ref=dst,
        send_sem=send_sem,
        recv_sem=recv_sem,
        device_id=on_dp(index),
        device_id_type=MESH,
    )


class Exchange:
    def __init__(self, n, place, device_of, src, dst, send_sem, recv_sem):
        self.n, self.place, self.device_of = n, place, device_of
        self.src, self.dst, self.send_sem, self.recv_sem = src, dst, send_sem, recv_sem

    def after(self, offset):
        return lax.rem(self.place + offset, self.n)

    def before(self, offset):
        return lax.rem(self.place + self.n - offset, self.n)

    def _out(self, offset):
        p = self.after(offset)
        return remote(
            self.src.at[p],
            self.dst.at[self.place],
            self.send_sem.at[p],
            self.recv_sem.at[self.place],
            self.device_of(p),
        )

    def start(self, offset):
        self._out(offset).start()

    def wait_send(self, offset):
        self._out(offset).wait_send()

    def wait_recv(self, offset):
        p = self.before(offset)
        remote(
            self.src.at[p], self.dst.at[p], self.send_sem.at[p], self.recv_sem.at[p], self.device_of(p)
        ).wait_recv()

    def each(self, method):
        @pl.loop(1, self.n)
        def _(offset):
            method(offset)

    def run(self):
        self.each(self.start)
        self.dst[self.place] = self.src[self.place]
        self.each(self.wait_recv)
        self.each(self.wait_send)


def greet(groups):
    barrier = pltpu.get_barrier_semaphore()
    total = 0
    for n, place, device_of in groups:
        @pl.loop(1, n)
        def _(offset):
            pl.semaphore_signal(
                barrier,
                inc=1,
                device_id=on_dp(device_of(lax.rem(place + offset, n))),
                device_id_type=MESH,
            )

        total += n - 1
    pl.semaphore_wait(barrier, total)


def swap_matrix(outer, inner, pair):
    n = outer * inner * pair
    row = lax.broadcasted_iota(jnp.int32, (n, n), 0)
    col = lax.broadcasted_iota(jnp.int32, (n, n), 1)
    i, o, r = row // (outer * pair), (row // pair) % outer, row % pair
    return (col == (o * inner + i) * pair + r).astype(jnp.bfloat16)


def swap_rows(outer, inner, pair, rows):
    return jnp.dot(
        swap_matrix(outer, inner, pair), rows, preferred_element_type=jnp.float32
    ).astype(jnp.bfloat16)


def slot_matrix(routes_ref, live_ref, slots, capacity):
    count = routes_ref.shape[1]
    target = routes_ref[...]
    row = lax.broadcasted_iota(jnp.int32, (count, count), 0)
    col = lax.broadcasted_iota(jnp.int32, (count, count), 1)
    wide = jnp.broadcast_to(target, (count, count))
    tall = jnp.sum(jnp.where(row == col, wide, 0), axis=1, keepdims=True)
    rank = jnp.sum(((tall == wide) & (row < col)).astype(jnp.int32), axis=0, keepdims=True)
    slot = target * capacity + rank
    alive = lax.broadcasted_iota(jnp.int32, (1, count), 1) < live_ref[...]
    slot = jnp.where(alive, slot, -1)
    return (lax.broadcasted_iota(jnp.int32, (slots, count), 0) == slot).astype(jnp.float32)


def dispatch_kernel(nz, capacity, frames_ref, routes_ref, live_ref, out_ref, sendz, recvz, sendj, recvj, sz, rz, sj, rj):
    me = lax.axis_index("dp")
    z, j = me // GROUP, lax.rem(me, GROUP)
    z_device = lambda p: p * GROUP + j
    j_device = lambda p: z * GROUP + p
    greet([(nz, z, z_device), (GROUP, j, j_device)])
    slots = nz * GROUP * capacity
    width = frames_ref.shape[1]
    hot = slot_matrix(routes_ref, live_ref, slots, capacity)
    empty = jnp.sum(hot, axis=1, keepdims=True) < 0.5
    rows = jnp.dot(hot.astype(jnp.bfloat16), frames_ref[...], preferred_element_type=jnp.float32)
    first = lax.broadcasted_iota(jnp.int32, (slots, width), 1) == 0
    rows = jnp.where(empty & first, ABSENT, rows).astype(jnp.bfloat16)
    sendz[...] = rows.reshape(sendz.shape)
    Exchange(nz, z, z_device, sendz, recvz, sz, rz).run()
    rows = swap_rows(nz, GROUP, capacity, recvz[...].reshape(slots, width))
    sendj[...] = rows.reshape(sendj.shape)
    Exchange(GROUP, j, j_device, sendj, recvj, sj, rj).run()
    out_ref[...] = swap_rows(GROUP, nz, capacity, recvj[...].reshape(slots, width))


def return_kernel(nz, capacity, rows_ref, routes_ref, live_ref, out_ref, sendj, recvj, sendz, recvz, sj, rj, sz, rz):
    me = lax.axis_index("dp")
    z, j = me // GROUP, lax.rem(me, GROUP)
    z_device = lambda p: p * GROUP + j
    j_device = lambda p: z * GROUP + p
    greet([(nz, z, z_device), (GROUP, j, j_device)])
    slots, width = rows_ref.shape
    sendj[...] = swap_rows(nz, GROUP, capacity, rows_ref[...]).reshape(sendj.shape)
    Exchange(GROUP, j, j_device, sendj, recvj, sj, rj).run()
    rows = swap_rows(GROUP, nz, capacity, recvj[...].reshape(slots, width))
    sendz[...] = rows.reshape(sendz.shape)
    Exchange(nz, z, z_device, sendz, recvz, sz, rz).run()
    hot = slot_matrix(routes_ref, live_ref, slots, capacity).astype(jnp.bfloat16)
    out_ref[...] = lax.dot_general(
        hot,
        recvz[...].reshape(slots, width),
        (((0,), (0,)), ((), ())),
        preferred_element_type=jnp.float32,
    ).astype(jnp.bfloat16)


def vmem_specs(n):
    return [pl.BlockSpec(memory_space=pltpu.VMEM)] * n


def move_rows(kernel, name, collective_id, out_rows, z_first, rows, routes_row, live, ndp, capacity):
    nz = ndp // GROUP
    width = rows.shape[1]
    by_z = pltpu.VMEM((nz, GROUP * capacity, width), jnp.bfloat16)
    by_j = pltpu.VMEM((GROUP, nz * capacity, width), jnp.bfloat16)
    dma = pltpu.SemaphoreType.DMA
    sems_z, sems_j = [dma((nz,))] * 2, [dma((GROUP,))] * 2
    scratch = [by_z, by_z, by_j, by_j] + sems_z + sems_j if z_first else [by_j, by_j, by_z, by_z] + sems_j + sems_z
    return pl.pallas_call(
        functools.partial(kernel, nz, capacity),
        out_shape=jax.ShapeDtypeStruct((out_rows, width), jnp.bfloat16),
        in_specs=vmem_specs(3),
        out_specs=vmem_specs(1)[0],
        scratch_shapes=scratch,
        compiler_params=pltpu.CompilerParams(
            collective_id=collective_id, has_side_effects=True, vmem_limit_bytes=24 * 1024 * 1024
        ),
        name=name,
    )(rows, routes_row, live)


def reduce_kernel(nz, grads_ref, act_ref, out_ref, mine, sib_out, sib_in, yx_out, yx_in, z_out, z_in, last_out, last_in, ss, rs, sy, ry, sz, rz, sl, rl):
    me = lax.axis_index("dp")
    nyx = GROUP // 2
    z, yx, core = me // GROUP, lax.rem(me, GROUP) // 2, lax.rem(me, 2)
    sibling = me + 1 - 2 * core
    z_device = lambda p: p * GROUP + yx * 2 + core
    yx_device = lambda p: z * GROUP + p * 2 + core
    core_device = lambda p: z * GROUP + yx * 2 + p
    greet([(nz, z, z_device), (nyx, yx, yx_device), (2, core, core_device)])
    tile, half = mine.shape[1], mine.shape[2]

    def product(p, which):
        rows = grads_ref[pl.ds(pl.multiple_of(p * tile, tile), tile), :]
        columns = pl.ds(pl.multiple_of(which * half, half), half)
        return 0.5 * jnp.dot(rows, act_ref[:, columns], preferred_element_type=jnp.float32)

    def to_sibling(p):
        return remote(sib_out.at[p], sib_in.at[p], ss.at[p], rs.at[p], sibling)

    @pl.loop(1, nyx + 1)
    def _(offset):
        p = lax.rem(yx + offset, nyx)
        sib_out[p] = product(p, 1 - core).astype(jnp.bfloat16)
        to_sibling(p).start()

    over_yx = Exchange(nyx, yx, yx_device, yx_out, yx_in, sy, ry)

    def add_cores(offset):
        p = lax.rem(yx + offset, nyx)
        to_sibling(p).wait_recv()
        return mine[p].astype(jnp.float32) + sib_in[p].astype(jnp.float32)

    @pl.loop(1, nyx + 1)
    def _(offset):
        p = lax.rem(yx + offset, nyx)
        mine[p] = product(p, core)

    @pl.loop(1, nyx)
    def _(offset):
        p = lax.rem(yx + offset, nyx)
        yx_out[p] = add_cores(offset).astype(jnp.bfloat16)
        over_yx.start(offset)

    mine[yx] = add_cores(nyx)

    @pl.loop(1, nyx)
    def _(offset):
        over_yx.wait_recv(offset)
        mine[yx] += yx_in[over_yx.before(offset)].astype(jnp.float32)

    z_out[...] = mine[yx].astype(jnp.bfloat16).reshape(z_out.shape)
    over_z = Exchange(nz, z, z_device, z_out, z_in, sz, rz)
    over_z.each(over_z.start)
    last_out[...] = z_out[z].astype(jnp.float32)

    @pl.loop(1, nz)
    def _(offset):
        over_z.wait_recv(offset)
        last_out[...] += z_in[over_z.before(offset)].astype(jnp.float32)

    last = remote(last_out, last_in, sl.at[0], rl.at[0], sibling)
    last.start()
    last.wait_recv()
    own, other = last_out[...], last_in[...]
    rows = own.shape[0] // 2
    is_low = core == 0
    own = jnp.where(is_low, own[:rows], own[rows:])
    other = jnp.where(is_low, other[:rows], other[rows:])
    out_ref[:, :half] = jnp.where(is_low, own, other)
    out_ref[:, half:] = jnp.where(is_low, other, own)
    last.wait_send()
    over_yx.each(over_yx.wait_send)
    over_z.each(over_z.wait_send)

    @pl.loop(0, nyx)
    def _(p):
        to_sibling(p).wait_send()


def reduce_grad(grads_turned, activated, ndp):
    nz, nyx = ndp // GROUP, GROUP // 2
    width, hidden_units = grads_turned.shape[0], activated.shape[1]
    tile, half, rows = width // nyx, hidden_units // 2, width // nyx // nz
    dma = pltpu.SemaphoreType.DMA
    wide = pltpu.VMEM((nyx, tile, half), jnp.bfloat16)
    thin = pltpu.VMEM((nz, rows, half), jnp.bfloat16)
    return pl.pallas_call(
        functools.partial(reduce_kernel, nz),
        out_shape=jax.ShapeDtypeStruct((rows // 2, hidden_units), jnp.float32),
        in_specs=vmem_specs(2),
        out_specs=vmem_specs(1)[0],
        scratch_shapes=[
            pltpu.VMEM((nyx, tile, half), jnp.float32),
            wide,
            wide,
            wide,
            wide,
            thin,
            thin,
            pltpu.VMEM((rows, half), jnp.float32),
            pltpu.VMEM((rows, half), jnp.float32),
            dma((nyx,)),
            dma((nyx,)),
            dma((nyx,)),
            dma((nyx,)),
            dma((nz,)),
            dma((nz,)),
            dma((1,)),
            dma((1,)),
        ],
        compiler_params=pltpu.CompilerParams(
            collective_id=3, has_side_effects=True, vmem_limit_bytes=32 * 1024 * 1024
        ),
        name="reduce_grad",
    )(grads_turned, activated)


def local(source_frames, routes, live_frames, norm_gain, weight_in, weight_out, cotangent):
    ndp, nt = lax.axis_size("dp"), lax.axis_size("tensor")
    capacity = cotangent.shape[0] // ndp
    width = cotangent.shape[1]
    nz = ndp // GROUP
    axes = ("dp", "tensor")
    partners = [(p * nt + t, (p ^ 2) * nt + (1 - t)) for p in range(ndp) for t in range(nt)]
    swap = lambda value: lax.ppermute(value, axes, partners)
    routes_row, live = routes.reshape(1, -1), live_frames.reshape(1, 1)

    cotangent_other = swap(cotangent)
    arrived = move_rows(
        dispatch_kernel, "dispatch", 1, ndp * capacity, True, source_frames, routes_row, live, ndp, capacity
    )
    arrived_other = swap(arrived)

    def normalise(slots):
        frames = slots.astype(jnp.float32)
        present = frames[:, :1] < 0.5 * ABSENT
        frames = jnp.where(present, frames, 0.0)
        centred = frames - jnp.mean(frames, axis=1, keepdims=True)
        inv_std = lax.rsqrt(jnp.mean(centred * centred, axis=1, keepdims=True) + epsilon)
        normed = centred * inv_std
        return present, frames, inv_std, normed, (normed * norm_gain).astype(jnp.bfloat16)

    def module(scaled, grads):
        hidden = jnp.dot(scaled, weight_in, preferred_element_type=jnp.float32)
        gate = jax.nn.sigmoid(hidden)
        activated = (hidden * gate).astype(jnp.bfloat16)
        grad_act = 0.5 * lax.dot_general(
            grads, weight_out, (((1,), (1,)), ((), ())), preferred_element_type=jnp.float32
        )
        grad_hidden = (grad_act * gate * (1.0 + hidden * (1.0 - gate))).astype(jnp.bfloat16)
        grad_scaled = lax.dot_general(
            grad_hidden, weight_in, (((1,), (1,)), ((), ())), preferred_element_type=jnp.float32
        ).astype(jnp.bfloat16)
        mixed_sum = jnp.dot(activated, weight_out, preferred_element_type=jnp.float32).astype(jnp.bfloat16)
        return activated, grad_scaled, mixed_sum

    present, frames, inv_std, normed, scaled = normalise(arrived)
    present_other, _, _, _, scaled_other = normalise(arrived_other)
    grads = jnp.where(present, cotangent, 0)
    grads_other = jnp.where(present_other, cotangent_other, 0)
    activated, grad_scaled, mixed_sum = module(scaled, grads)
    activated_other, grad_scaled_other, mixed_sum_other = module(scaled_other, grads_other)
    grad_scaled_back = swap(grad_scaled_other)
    mixed_back = swap(mixed_sum_other)

    both = jnp.concatenate([grads, grads_other], axis=0)
    turned = both.reshape(-1, nz, GROUP // 2, width // nz // (GROUP // 2)).transpose(2, 1, 3, 0).reshape(width, -1)
    grad_out = reduce_grad(turned, jnp.concatenate([activated, activated_other], axis=0), ndp).T

    grad_normed = (grad_scaled.astype(jnp.float32) + grad_scaled_back.astype(jnp.float32)) * norm_gain
    first_mean = jnp.mean(grad_normed, axis=1, keepdims=True)
    second_mean = jnp.mean(grad_normed * normed, axis=1, keepdims=True)
    grad_rows = (
        grads.astype(jnp.float32) + inv_std * (grad_normed - first_mean - normed * second_mean)
    ).astype(jnp.bfloat16)
    grad_source = move_rows(
        return_kernel, "give_back", 2, source_frames.shape[0], False, grad_rows, routes_row, live, ndp, capacity
    )
    mixed = (
        frames + 0.5 * (mixed_sum.astype(jnp.float32) + mixed_back.astype(jnp.float32))
    ).astype(jnp.bfloat16)
    return (mixed, grad_source, grad_out)


def solution(mesh):
    return jax.shard_map(
        local,
        mesh=mesh,
        in_specs=(
            P(("dp", "tensor"), None),
            P(("dp", "tensor"), None),
            P(("dp", "tensor")),
            P(),
            P(None, "tensor"),
            P("tensor", None),
            P(("dp", "tensor"), None),
        ),
        out_specs=(P(("dp", "tensor"), None), P(("dp", "tensor"), None), P("tensor", "dp")),
        check_vma=False,
    )
```

time: 703 us -> 187 us (0.27)
  blocking collectives: 390 us -> 0 us
  Pallas kernels: 0 us -> 121 us
  starting transfers between devices: 118 us -> 6.35 us
  waiting for transfers between devices: 87.7 us -> 14.9 us
  local copies, waits for them, and re-layouts: 39.5 us -> 7.71 us
  between operations: 16.1 us -> 1.48 us
  other arithmetic: 14 us -> 2.48 us
    unnamed x1 -> x0, blocking collectives: 334 us -> none
    pallas_call x0 -> x3, Pallas kernels: none -> 121 us  [the longest x2 74.6 us: move_rows(): pl.pallas_call(functools.partial(kernel, nz, capacity), out_shape=jax.Sha...]
    unnamed x32 -> x0, starting transfers between devices: 105 us -> none
    all_to_all x2 -> x0, blocking collectives: 55.7 us -> none  [the longest x1 38.6 us: local(): lax.all_to_all(outgoing, 'dp', split_axis=0, concat_axis=0, tiled=True)]
    reduce_scatter x2 -> x0, waiting for transfers between devices: 49.5 us -> none  [the longest x1 33.1 us: local(): lax.psum_scatter(jnp.dot(piece, weight_out, preferred_element_type=jnp.fl...]
    all_gather x2 -> x0, waiting for transfers between devices: 37.8 us -> none  [the longest x1 27.4 us: local(): grad_all = lax.all_gather(grad_rows, 'tensor', axis=0, tiled=True)]
    unnamed x68 -> x26, local copies, waits for them, and re-layouts: 32.7 us -> 4.45 us
    ppermute x0 -> x4, waiting for transfers between devices: none -> 14.9 us  [local(): swap = lambda value: lax.ppermute(value, axes, partners)]
  transfers between devices with their start and end apart: 37 -> 4, of which waited for: 5 -> 1; matrix products, arithmetic and copies ran while one was open for 56% -> 12% of each run, Pallas kernels for 0% -> 46%
where the time goes in v1:
time: 187 us; the launch traced here: 186 us
  Pallas kernels  121 us (65%)
  matrix products  32.5 us (17%)
  waiting for transfers between devices  14.9 us (8%)
  local copies, waits for them, and re-layouts  7.71 us (4%)
  starting transfers between devices  6.35 us (3%)
  other arithmetic  2.48 us (1%)
    pallas_call x2, Pallas kernels, move_rows(): pl.pallas_call(functools.partial(kernel, nz, capacity), out_shape=jax.Sha...  74.6 us
    pallas_call x1, Pallas kernels, reduce_grad(): pl.pallas_call(functools.partial(reduce_kernel, nz), out_shape=jax.ShapeD...  46.5 us
    dot_general x2, matrix products, module(): lax.dot_general(grad_hidden, weight_in, (((1,), (1,)), ((), ())), preferr...  16.4 us
    ppermute x4, waiting for transfers between devices, local(): swap = lambda value: lax.ppermute(value, axes, partners)  14.9 us
    dot_general x2, matrix products, module(): jnp.dot(activated, weight_out, preferred_element_type=jnp.float32)  10.3 us
    ppermute x4, starting transfers between devices, local(): swap = lambda value: lax.ppermute(value, axes, partners)  6.35 us
    dot_general x2, matrix products, module(): hidden = jnp.dot(scaled, weight_in, preferred_element_type=jnp.float32)  5.75 us
    unnamed x26, local copies, waits for them, and re-layouts  4.45 us
  transfers between devices with their start and end apart: 4, of which 1 were waited for; matrix products, arithmetic and copies ran while one was open for 12% of the time, Pallas kernels for 46%

profile of v1, /device:TPU:1, one launch (start us, length us, event | category | flops | bytes accessed | tf_op | source)
XLA Modules:
  0.0 186.4 jit_solution(8176264478426452293)
XLA Ops:
  0.6 3.4 %collective-permute-start.2 = (bf16[256,1536]{1,0:T(8,128)(2,1)}, bf16[256,1536]{1,0:T(8,128)(2,1)S(1)}, u32[]{:S(2)}, u32[]{:S(2)}) collective-permute-start(bf16[256,1536]{1,0:T(8,128)(2,1)} %param.13), channel_id=1, source_target_pairs={{0,5},{1,4},{2,7},{3,6},{4,1},{5,0},{6,3},{7,2},{8,13},{9,12},{10,... | collective-permute-start | bytes 2359304 | tf_op jit(solution)/shard_map/ppermute | solution.py:312
  4.7 1.0 copy-done
  5.7 0.7 copy-done.1
  6.3 39.3 %dispatch.1 = bf16[256,1536]{1,0:T(8,128)(2,1)S(1)} custom-call(bf16[128,1536]{1,0:T(8,128)(2,1)S(1)} %copy-done, s32[1,128]{1,0:T(1,128)S(1)} %bitcast.22, s32[1,1]{1,0:T(1,128)} %bitcast.18.live_ref), custom_call_target="tpu_custom_call" | custom-call | tf_op jit(solution)/shard_map/dispatch/pallas_call | solution.py:175
  45.7 0.3 collective-permute-start
  46.3 0.3 select_reduce_fusion.1
  46.9 0.4 multiply_reduce_fusion.2
  47.3 1.0 copy-done.10
  48.4 3.0 %multiply_convert_fusion.2 = (bf16[256,1536]{1,0:T(8,128)(2,1)}, f32[256,1536]{1,0:T(8,128)}) fusion(bf16[1536,1536]{1,0:T(8,128)(2,1)S(1)} %copy-done.10, bf16[256,1536]{1,0:T(8,128)(2,1)S(1)} %dispatch.1, f32[1536]{0:T(1024)S(1)} %copy-done.11, f32[256]{0:T(256)S(1)} %add_rsqrt_fusion.1, f32[256]{0:T(256)S(1)} %broadcast_multiply_fusion.3, ...), kind=kOutput, calls=%fused_computation.24 | convolution fusion | flops 1212284928 | bytes 7872768 | tf_op jit(solution)/shard_map/dot_general | solution.py:331
  51.3 14.9 %collective-permute-done = bf16[256,1536]{1,0:T(8,128)(2,1)S(1)} collective-permute-done((bf16[256,1536]{1,0:T(8,128)(2,1)S(1)}, bf16[256,1536]{1,0:T(8,128)(2,1)S(1)}, u32[]{:S(2)}, u32[]{:S(2)}) %collective-permute-start) | collective-permute-done | bytes 786464 | tf_op jit(solution)/shard_map/ppermute | solution.py:312
  66.5 0.3 select_reduce_fusion
  66.8 0.4 multiply_reduce_fusion.1
  67.4 2.8 %multiply_convert_fusion = (bf16[256,1536]{1,0:T(8,128)(2,1)S(1)}, f32[256,1536]{1,0:T(8,128)}) fusion(bf16[1536,1536]{1,0:T(8,128)(2,1)S(1)} %copy-done.10, bf16[256,1536]{1,0:T(8,128)(2,1)S(1)} %collective-permute-done, f32[256]{0:T(256)S(1)} %add_rsqrt_fusion, f32[256]{0:T(256)S(1)} %broadcast_multiply_fusion.2, f32[1536]{0:T(1024)S(1)} %copy-done.11, ...), kind=kOutput, calls=%fused_computation.20 | convolution fusion | flops 1212284928 | bytes 7872768 | tf_op jit(solution)/shard_map/dot_general | solution.py:331
  70.2 8.1 %convolution_convert_fusion = bf16[256,1536]{1,0:T(8,128)(2,1)} fusion(bf16[1536,1536]{1,0:T(8,128)(2,1)} %param.11, bf16[256,1536]{1,0:T(8,128)(2,1)S(1)} %broadcast_select_fusion, bf16[1536,1536]{1,0:T(8,128)(2,1)} %param.12, f32[256,1536]{1,0:T(8,128)} %get-tuple-element.11), kind=kOutput, calls=%fused_computation.8 | convolution fusion | flops 2420244480 | bytes 12582912 | tf_op jit(solution)/shard_map/dot_general | solution.py:338
  78.3 4.7 %convolution_convert_fusion.2 = bf16[256,1536]{1,0:T(8,128)(2,1)} fusion(bf16[256,1536]{1,0:T(8,128)(2,1)S(1)} %get-tuple-element.10, bf16[1536,1536]{1,0:T(8,128)(2,1)} %param.12), kind=kOutput, calls=%fused_computation.11 | convolution fusion | flops 1208352768 | bytes 6291456 | tf_op jit(solution)/shard_map/dot_general | solution.py:341
  83.0 2.7 %collective-permute-start.1 = (bf16[256,1536]{1,0:T(8,128)(2,1)}, bf16[256,1536]{1,0:T(8,128)(2,1)}, u32[]{:S(2)}, u32[]{:S(2)}) collective-permute-start(bf16[256,1536]{1,0:T(8,128)(2,1)} %convolution_convert_fusion.2), channel_id=1, source_target_pairs={{0,5},{1,4},{2,7},{3,6},{4,1},{5,0},{6,3},{7,2},{8,13},{9,12},{10,... | collective-permute-start | bytes 2359304 | tf_op jit(solution)/shard_map/ppermute | solution.py:312
  85.7 1.6 copy.11
  87.3 1.7 copy.12
  89.3 46.5 %reduce_grad.1 = f32[12,1536]{1,0:T(8,128)S(1)} custom-call(bf16[1536,512]{1,0:T(8,128)(2,1)S(1)} %bitcast.20, bf16[512,1536]{1,0:T(8,128)(2,1)S(1)} %pad_maximum_fusion.1.act_ref), custom_call_target="tpu_custom_call" | custom-call | tf_op jit(solution)/shard_map/reduce_grad/pallas_call | solution.py:274
  135.8 8.3 %fusion.28 = (f32[256]{0:T(256)S(1)}, f32[256]{0:T(256)S(1)}, f32[256,1536]{1,0:T(8,128)}) fusion(f32[256]{0:T(256)S(1)} %add_rsqrt_fusion.1, f32[256]{0:T(256)S(1)} %broadcast_multiply_fusion.3, bf16[256,1536]{1,0:T(8,128)(2,1)S(1)} %dispatch.1, pred[256]{0:T(512)(128)(4,1)S(1)} %fusion.20, f32[1536]{0:T(1024)S(1)} %copy-done.11, ...), kind=kOutput, calls=%fused_computation.61 | convolution fusion | flops 2424962560 | bytes 14952704 | tf_op jit(solution)/shard_map/dot_general | solution.py:338
  144.1 5.6 %add_convert_fusion = (bf16[256,1536]{1,0:T(8,128)(2,1)S(1)}, bf16[256,1536]{1,0:T(8,128)(2,1)}) fusion(f32[256,1536]{1,0:T(8,128)} %get-tuple-element.7, bf16[256,1536]{1,0:T(8,128)(2,1)S(1)} %dispatch.1, f32[256]{0:T(256)S(1)} %get-tuple-element.12, f32[256]{0:T(256)S(1)} %get-tuple-element.13, f32[256]{0:T(256)S(1)} %add_rsqrt_fusion.1, ...), kind=kOutput, calls=%fused_computation.16 | convolution fusion | flops 1215430656 | bytes 11014400 | tf_op jit(solution)/shard_map/dot_general | solution.py:341
  149.8 35.3 %give_back.1 = bf16[128,1536]{1,0:T(8,128)(2,1)S(1)} custom-call(bf16[256,1536]{1,0:T(8,128)(2,1)S(1)} %get-tuple-element.5.rows_ref, s32[1,128]{1,0:T(1,128)S(1)} %bitcast.23, s32[1,1]{1,0:T(1,128)} %bitcast.19.live_ref), custom_call_target="tpu_custom_call" | custom-call | tf_op jit(solution)/shard_map/give_back/pallas_call | solution.py:175
  185.0 0.7 copy.16
  185.8 0.6 copy.17
  (38 shorter events, 1.5 us)
Async XLA Ops:
  0.6 66.6 %collective-permute-start.2 = (bf16[256,1536]{1,0:T(8,128)(2,1)}, bf16[256,1536]{1,0:T(8,128)(2,1)S(1)}, u32[]{:S(2)}, u32[]{:S(2)}) collective-permute-start(bf16[256,1536]{1,0:T(8,128)(2,1)} %param.13), channel_id=1, source_target_pairs={{0,5},{1,4},{2,7},{3,6},{4,1},{5,0},{6,3},{7,2},{8,13},{9,12},{10,... | collective-permute-start | bytes 2359304 | tf_op jit(solution)/shard_map/ppermute | solution.py:312
  4.7 1.0 copy-start
  5.7 0.7 copy-start.1
  45.7 1.1 copy-start.5
  45.7 20.6 %collective-permute-start = (bf16[256,1536]{1,0:T(8,128)(2,1)S(1)}, bf16[256,1536]{1,0:T(8,128)(2,1)S(1)}, u32[]{:S(2)}, u32[]{:S(2)}) collective-permute-start(bf16[256,1536]{1,0:T(8,128)(2,1)S(1)} %dispatch.1), channel_id=1, source_target_pairs={{0,5},{1,4},{2,7},{3,6},{4,1},{5,0},{6,3},{7,2},{8,13},{9,12},{10,... | collective-permute-start | bytes 2359304 | tf_op jit(solution)/shard_map/ppermute | solution.py:312
  46.0 2.4 %copy-start.10 = (bf16[1536,1536]{1,0:T(8,128)(2,1)S(1)}, bf16[1536,1536]{1,0:T(8,128)(2,1)}, u32[]{:S(2)}) copy-start(bf16[1536,1536]{1,0:T(8,128)(2,1)} %param.11) | copy-start | bytes 14155780
  46.2 2.1 %copy-start.11 = (f32[1536]{0:T(1024)S(1)}, f32[1536]{0:T(1024)}, u32[]{:S(2)}) copy-start(f32[1536]{0:T(1024)} %param.10) | copy-start | bytes 18436
  67.4 2.8 %copy-start.3 = (bf16[256,1536]{1,0:T(8,128)(2,1)}, bf16[256,1536]{1,0:T(8,128)(2,1)S(1)}, u32[]{:S(2)}) copy-start(bf16[256,1536]{1,0:T(8,128)(2,1)S(1)} %broadcast_select_fusion) | copy-start | bytes 2359300
  70.2 8.1 %copy-start.8 = (bf16[256,1536]{1,0:T(8,128)(2,1)}, bf16[256,1536]{1,0:T(8,128)(2,1)S(1)}, u32[]{:S(2)}) copy-start(bf16[256,1536]{1,0:T(8,128)(2,1)S(1)} %get-tuple-element.10) | copy-start | bytes 2359300
  78.3 57.5 %collective-permute-start.3 = (bf16[256,1536]{1,0:T(8,128)(2,1)}, bf16[256,1536]{1,0:T(8,128)(2,1)}, u32[]{:S(2)}, u32[]{:S(2)}) collective-permute-start(bf16[256,1536]{1,0:T(8,128)(2,1)} %convolution_convert_fusion), channel_id=1, source_target_pairs={{0,5},{1,4},{2,7},{3,6},{4,1},{5,0},{6,3},{7,2},{8,13},{9,12},{10,... | collective-permute-start | bytes 2359304 | tf_op jit(solution)/shard_map/ppermute | solution.py:312
  78.3 7.4 %copy-start.4 = (bf16[256,1536]{1,0:T(8,128)(2,1)S(1)}, bf16[256,1536]{1,0:T(8,128)(2,1)}, u32[]{:S(2)}) copy-start(bf16[256,1536]{1,0:T(8,128)(2,1)} %copy-done.3) | copy-start | bytes 2359300
  83.0 61.2 %collective-permute-start.1 = (bf16[256,1536]{1,0:T(8,128)(2,1)}, bf16[256,1536]{1,0:T(8,128)(2,1)}, u32[]{:S(2)}, u32[]{:S(2)}) collective-permute-start(bf16[256,1536]{1,0:T(8,128)(2,1)} %convolution_convert_fusion.2), channel_id=1, source_target_pairs={{0,5},{1,4},{2,7},{3,6},{4,1},{5,0},{6,3},{7,2},{8,13},{9,12},{10,... | collective-permute-start | bytes 2359304 | tf_op jit(solution)/shard_map/ppermute | solution.py:312
  87.3 1.7 copy-start.7
  87.3 1.8 copy-start.9
  89.3 46.5 %copy-start.6 = (bf16[256,1536]{1,0:T(8,128)(2,1)S(1)}, bf16[256,1536]{1,0:T(8,128)(2,1)}, u32[]{:S(2)}) copy-start(bf16[256,1536]{1,0:T(8,128)(2,1)} %param.13) | copy-start | bytes 2359300
  144.1 5.6 %copy-start.2 = (s32[128,1]{0,1:T(1,128)S(1)}, s32[128,1]{0,1:T(1,128)}, u32[]{:S(2)}) copy-start(s32[128,1]{0,1:T(1,128)} %param.8) | copy-start | bytes 1540

commit v2 on v0

v2 whole, which is shorter than its diff:
```python
import functools
from types import SimpleNamespace

import jax
import jax.numpy as jnp
from jax import lax
from jax.experimental import pallas as pl
from jax.experimental.pallas import tpu as pltpu
from jax.sharding import PartitionSpec as P

epsilon = 1e-05
ABSENT = 64.0
MESH = pl.DeviceIdType.MESH
GROUP = 16
RING = 4
DMA = pltpu.SemaphoreType.DMA
BF16, F32 = jnp.bfloat16, jnp.float32


def remote(src, dst, send_sem, recv_sem, device):
    return pltpu.make_async_remote_copy(
        src_ref=src, dst_ref=dst, send_sem=send_sem, recv_sem=recv_sem, device_id=device, device_id_type=MESH
    )


class Exchange:
    def __init__(self, n, place, device_of, buffers):
        self.n, self.place, self.device_of = n, place, device_of
        self.src, self.dst, self.send_sem, self.recv_sem = buffers

    def _out(self, offset):
        p = lax.rem(self.place + offset, self.n)
        return remote(
            self.src.at[p], self.dst.at[self.place], self.send_sem.at[p], self.recv_sem.at[self.place], self.device_of(p)
        )

    def start(self):
        @pl.loop(1, self.n)
        def _(offset):
            self._out(offset).start()

        self.dst[self.place] = self.src[self.place]

    def wait_recv(self):
        @pl.loop(1, self.n)
        def _(offset):
            p = lax.rem(self.place + offset, self.n)
            remote(
                self.src.at[p], self.dst.at[p], self.send_sem.at[p], self.recv_sem.at[p], self.device_of(p)
            ).wait_recv()

    def wait_send(self):
        @pl.loop(1, self.n)
        def _(offset):
            self._out(offset).wait_send()


def swap_rows(outer, inner, rows):
    n = outer * inner
    row = lax.broadcasted_iota(jnp.int32, (n, n), 0)
    col = lax.broadcasted_iota(jnp.int32, (n, n), 1)
    matrix = (col == lax.rem(row, outer) * inner + row // outer).astype(BF16)
    return jnp.dot(matrix, rows, preferred_element_type=F32).astype(BF16)


def slot_matrix(routes_ref, live_ref, ndp, capacity):
    count = routes_ref.shape[1]
    target = routes_ref[...]
    row = lax.broadcasted_iota(jnp.int32, (count, count), 0)
    col = lax.broadcasted_iota(jnp.int32, (count, count), 1)
    wide = jnp.broadcast_to(target, (count, count))
    tall = jnp.sum(jnp.where(row == col, wide, 0), axis=1, keepdims=True)
    rank = jnp.sum(((tall == wide) & (row < col)).astype(jnp.int32), axis=0, keepdims=True)
    alive = lax.broadcasted_iota(jnp.int32, (1, count), 1) < live_ref[...]
    slot = jnp.where(alive, rank * ndp + target, -1)
    return (lax.broadcasted_iota(jnp.int32, (ndp * capacity, count), 0) == slot).astype(F32)


def dot_t(left, right):
    return lax.dot_general(left, right, (((1,), (1,)), ((), ())), preferred_element_type=F32)


def t_dot(left, right):
    return lax.dot_general(left, right, (((0,), (0,)), ((), ())), preferred_element_type=F32)


def tiles(total, size, body):
    @pl.loop(0, total // size)
    def _(i):
        body(pl.ds(pl.multiple_of(i * size, size), size))


def kernel(ndp, names, *refs):
    r = SimpleNamespace(**dict(zip(names, refs)))
    me, t = lax.axis_index("dp"), lax.axis_index("tensor")
    nz = ndp // GROUP
    z, j = me // GROUP, lax.rem(me, GROUP)
    y, yx, xl, core = j // 4, j // 2, lax.rem(j // 2, 2), lax.rem(j, 2)
    z_device = lambda p: {"dp": p * GROUP + j}
    j_device = lambda p: {"dp": z * GROUP + p}
    y_device = lambda p: {"dp": z * GROUP + p * 4 + xl * 2 + core}
    x_device = {"dp": me + 2 - 4 * xl}
    sibling = {"dp": me + 1 - 2 * core}
    partner = {"dp": me + 2 - 4 * xl, "tensor": 1 - t}
    width = r.source.shape[1]
    units = r.win.shape[1]
    half = units // 2

    load_in = pltpu.make_async_copy(r.weight_in, r.win, r.load_sem.at[0])
    load_out = pltpu.make_async_copy(r.weight_out, r.wout, r.load_sem.at[1])
    load_in.start()
    load_out.start()

    barrier = pltpu.get_barrier_semaphore()

    @pl.loop(1, nz)
    def _(offset):
        pl.semaphore_signal(barrier, inc=1, device_id=z_device(lax.rem(z + offset, nz)), device_id_type=MESH)

    @pl.loop(1, GROUP)
    def _(offset):
        pl.semaphore_signal(barrier, inc=1, device_id=j_device(lax.rem(j + offset, GROUP)), device_id_type=MESH)

    pl.semaphore_signal(barrier, inc=1, device_id=partner, device_id_type=MESH)

    hot = slot_matrix(r.routes, r.live, ndp, 2)
    r.hot[...] = hot.astype(BF16)
    first = lax.broadcasted_iota(jnp.int32, (ndp, width), 1) == 0

    def outgoing(rank):
        part = hot[rank * ndp : (rank + 1) * ndp]
        empty = jnp.sum(part, axis=1, keepdims=True) < 0.5
        rows = jnp.dot(part.astype(BF16), r.source[...], preferred_element_type=F32)
        return jnp.where(empty & first, ABSENT, rows).astype(BF16)

    def exchanges(prefix):
        bufs = lambda name: tuple(getattr(r, prefix + name + end) for end in ("_out", "_in", "_ss", "_rs"))
        over_z = lambda name: Exchange(nz, z, z_device, bufs(name))
        over_j = lambda name: Exchange(GROUP, j, j_device, bufs(name))
        return over_z("z0"), over_j("j0"), over_j("j1"), over_z("z1")

    z0, j0, j1, z1 = exchanges("a")
    z0.src[...] = outgoing(0).reshape(z0.src.shape)
    j1.src[...] = swap_rows(nz, GROUP, outgoing(1)).reshape(j1.src.shape)
    pl.semaphore_wait(barrier, nz + GROUP - 1)
    z0.start()
    j1.start()

    def across(name, c):
        out, land, ss, rs = (getattr(r, name + end) for end in ("_out", "_in", "_ss", "_rs"))
        return remote(out.at[c], land.at[c], ss.at[c], rs.at[c], partner)

    cot_copy = remote(r.cot, r.cot_in, r.cot_sem.at[0], r.cot_sem.at[1], partner)
    cot_copy.start()
    r.grads[: 2 * ndp] = swap_rows(ndp, 2, r.cot[...])
    load_in.wait()
    load_out.wait()

    def process(k):
        rows = pl.ds(k * ndp, ndp)
        slots = (r.fr_out if k < 2 else r.fr_in)[k % 2].astype(F32)
        present = slots[:, :1] < 0.5 * ABSENT
        frames = jnp.where(present, slots, 0.0)
        centred = frames - jnp.mean(frames, axis=1, keepdims=True)
        inv_std = lax.rsqrt(jnp.mean(centred * centred, axis=1, keepdims=True) + epsilon)
        normed = centred * inv_std
        if k < 2:
            r.normed[k] = normed
            r.inv_std[k] = inv_std
        r.scaled[...] = (normed * r.gain[...]).astype(BF16)
        r.grads[rows] = jnp.where(present, r.grads[rows].astype(F32), 0.0).astype(BF16)

        def tile(n):
            hidden = jnp.dot(r.scaled[...], r.win[:, n], preferred_element_type=F32)
            grad_act = 0.5 * dot_t(r.grads[rows], r.wout[n, :])
            gate = jax.nn.sigmoid(hidden)
            r.act[rows, n] = (hidden * gate).astype(BF16)
            r.gh[rows, n] = (grad_act * gate * (1.0 + hidden * (1.0 - gate))).astype(BF16)

        tiles(units, 512, tile)

    def scaled_grad(k, out, c):
        def tile(n):
            out[c, :, n] = dot_t(r.gh[pl.ds(k * ndp, ndp), :], r.win[n, :]).astype(BF16)

        tiles(width, 512, tile)

    def mix(k, out, c):
        def tile(n):
            out[c, :, n] = jnp.dot(
                r.act[pl.ds(k * ndp, ndp), :], r.wout[:, n], preferred_element_type=F32
            ).astype(BF16)

        tiles(width, 512, tile)

    j1.wait_recv()
    z1.src[...] = swap_rows(GROUP, nz, j1.dst[...].reshape(ndp, width)).reshape(z1.src.shape)
    z1.start()
    z0.wait_recv()
    j0.src[...] = swap_rows(nz, GROUP, z0.dst[...].reshape(ndp, width)).reshape(j0.src.shape)
    j0.start()
    j0.wait_recv()
    r.fr_out[0] = swap_rows(GROUP, nz, j0.dst[...].reshape(ndp, width))
    across("fr", 0).start()
    process(0)
    z1.wait_recv()
    r.fr_out[1] = z1.dst[...].reshape(ndp, width)
    across("fr", 1).start()
    process(1)
    cot_copy.wait_recv()
    r.grads[2 * ndp :] = swap_rows(ndp, 2, r.cot_in[...])
    across("fr", 0).wait_recv()
    process(2)
    scaled_grad(2, r.gs_out, 0)
    across("gs", 0).start()
    across("fr", 1).wait_recv()
    process(3)
    scaled_grad(3, r.gs_out, 1)
    across("gs", 1).start()

    rows_of_z = width // nz
    pair = 2 * rows_of_z
    shape = (2,) + r.mine.shape[1:]

    def product(i, which):
        columns = pl.ds(pl.multiple_of(which * half, half), half)
        left = r.grads[:, pl.ds(pl.multiple_of(i * pair, pair), pair)]
        return (0.5 * t_dot(left, r.act[:, columns])).reshape(shape)

    def to_sibling(i):
        part = pl.ds(2 * i, 2)
        return remote(r.sib_out.at[part], r.sib_in.at[part], r.sib_ss.at[i], r.sib_rs.at[i], sibling)

    @pl.loop(0, nz // 2)
    def _(i):
        r.sib_out[pl.ds(2 * i, 2)] = product(i, 1 - core).astype(BF16)
        to_sibling(i).start()

    @pl.loop(0, nz // 2)
    def _(i):
        r.mine[pl.ds(2 * i, 2)] = product(i, core)

    scaled_grad(0, r.gs_own, 0)
    scaled_grad(1, r.gs_own, 1)

    @pl.loop(0, nz // 2)
    def _(i):
        to_sibling(i).wait_recv()

    up, down, opposite = lax.rem(y + 1, RING), lax.rem(y + 3, RING), lax.rem(y + 2, RING)

    def cores(y_at, x_at):
        p = y_at * 2 + x_at
        return r.mine[:, p] + r.sib_in[:, p].astype(F32)

    def along(name, slot):
        out, land, ss, rs = (getattr(r, name + end) for end in ("_out", "_in", "_ss", "_rs"))
        to_up = slot == 0 if name == "y1" else slot < 2
        return remote(
            out.at[slot], land.at[slot], ss.at[slot], rs.at[slot], y_device(up) if to_up else y_device(down)
        )

    r.y1_out[0] = cores(opposite, 0).astype(BF16)
    along("y1", 0).start()
    r.y1_out[1] = cores(opposite, 1).astype(BF16)
    along("y1", 1).start()
    r.y2_out[1] = cores(up, 1).astype(BF16)
    along("y2", 1).start()
    r.y2_out[2] = cores(down, 0).astype(BF16)
    along("y2", 2).start()
    mix(2, r.mx_out, 0)
    mix(3, r.mx_out, 1)
    along("y1", 0).wait_recv()
    r.y2_out[0] = (cores(up, 0) + r.y1_in[0].astype(F32)).astype(BF16)
    along("y2", 0).start()
    along("y1", 1).wait_recv()
    r.y2_out[3] = (cores(down, 1) + r.y1_in[1].astype(F32)).astype(BF16)
    along("y2", 3).start()

    def gradient(c):
        normed = r.normed[c]
        g = (r.gs_own[c].astype(F32) + r.gs_in[c].astype(F32)) * r.gain[...]
        first_mean = jnp.mean(g, axis=1, keepdims=True)
        second_mean = jnp.mean(g * normed, axis=1, keepdims=True)
        own = r.grads[pl.ds(c * ndp, ndp)].astype(F32)
        return (own + r.inv_std[c] * (g - first_mean - normed * second_mean)).astype(BF16)

    z2, j2, j3, z3 = exchanges("b")
    across("gs", 0).wait_recv()
    z2.src[...] = gradient(0).reshape(z2.src.shape)
    z2.start()
    across("gs", 1).wait_recv()
    j3.src[...] = swap_rows(nz, GROUP, gradient(1)).reshape(j3.src.shape)
    j3.start()
    across("mx", 0).start()
    across("mx", 1).start()
    mix(0, r.mx_own, 0)
    mix(1, r.mx_own, 1)

    for slot in range(4):
        along("y2", slot).wait_recv()
    for x_at in range(2):
        r.total[x_at] = cores(y, x_at) + r.y2_in[x_at].astype(F32) + r.y2_in[2 + x_at].astype(F32)
    r.x_out[...] = r.total[1 - xl].astype(BF16)
    x_copy = remote(r.x_out, r.x_in, r.x_sem.at[0], r.x_sem.at[1], x_device)
    x_copy.start()

    j3.wait_recv()
    z3.src[...] = swap_rows(GROUP, nz, j3.dst[...].reshape(ndp, width)).reshape(z3.src.shape)
    z3.start()
    z2.wait_recv()
    j2.src[...] = swap_rows(nz, GROUP, z2.dst[...].reshape(ndp, width)).reshape(j2.src.shape)
    j2.start()

    x_copy.wait_recv()
    over_z = Exchange(nz, z, z_device, (r.zr_out, r.zr_in, r.zr_ss, r.zr_rs))
    r.zr_out[...] = (r.total[xl] + r.x_in[...].astype(F32)).astype(BF16)
    over_z.start()

    j2.wait_recv()
    given = t_dot(r.hot[:ndp], swap_rows(GROUP, nz, j2.dst[...].reshape(ndp, width)))
    over_z.wait_recv()
    r.last_out[...] = jnp.sum(r.zr_in[...].astype(F32), axis=0)
    last = remote(r.last_out, r.last_in, r.last_sem.at[0], r.last_sem.at[1], sibling)
    last.start()

    for c in range(2):
        across("mx", c).wait_recv()
    mixed_rows = []
    for c in range(2):
        slots = r.fr_out[c].astype(F32)
        frames = jnp.where(slots[:, :1] < 0.5 * ABSENT, slots, 0.0)
        mixed_rows.append((frames + 0.5 * (r.mx_own[c].astype(F32) + r.mx_in[c].astype(F32))).astype(BF16))
    r.mixed[...] = swap_rows(2, ndp, jnp.concatenate(mixed_rows, axis=0))

    z3.wait_recv()
    given += t_dot(r.hot[ndp:], z3.dst[...].reshape(ndp, width))
    r.grad_source[...] = given.astype(BF16)

    last.wait_recv()
    own, other = r.last_out[...], r.last_in[...]
    count = own.shape[0] // 2
    is_low = core == 0
    own = jnp.where(is_low, own[:count], own[count:])
    other = jnp.where(is_low, other[:count], other[count:])
    r.grad_out[:, :half] = jnp.where(is_low, own, other)
    r.grad_out[:, half:] = jnp.where(is_low, other, own)

    last.wait_send()
    x_copy.wait_send()
    cot_copy.wait_send()
    for exchange in (z0, j0, j1, z1, z2, j2, j3, z3, over_z):
        exchange.wait_send()
    for name in ("fr", "gs", "mx"):
        for c in range(2):
            across(name, c).wait_send()
    for slot in range(2):
        along("y1", slot).wait_send()
    for slot in range(4):
        along("y2", slot).wait_send()

    @pl.loop(0, nz // 2)
    def _(i):
        to_sibling(i).wait_send()


def local(source_frames, routes, live_frames, norm_gain, weight_in, weight_out, cotangent):
    ndp = lax.axis_size("dp")
    nz = ndp // GROUP
    width, units = weight_in.shape
    half, strip = units // 2, width // ndp * 2
    vmem = pltpu.VMEM
    inputs = {
        "source": source_frames,
        "routes": routes.reshape(1, -1),
        "live": live_frames.reshape(1, 1),
        "gain": norm_gain.reshape(1, -1),
        "cot": cotangent,
        "weight_in": weight_in,
        "weight_out": weight_out,
    }
    outputs = {
        "mixed": jax.ShapeDtypeStruct(cotangent.shape, BF16),
        "grad_source": jax.ShapeDtypeStruct(source_frames.shape, BF16),
        "grad_out": jax.ShapeDtypeStruct((width // ndp, units), F32),
    }
    scratch = {
        "win": vmem(weight_in.shape, BF16),
        "wout": vmem(weight_out.shape, BF16),
        "load_sem": DMA((2,)),
        "hot": vmem((2 * ndp, source_frames.shape[0]), BF16),
        "cot_in": vmem(cotangent.shape, BF16),
        "cot_sem": DMA((2,)),
        "grads": vmem((4 * ndp, width), BF16),
        "act": vmem((4 * ndp, units), BF16),
        "gh": vmem((4 * ndp, units), BF16),
        "scaled": vmem((ndp, width), BF16),
        "normed": vmem((2, ndp, width), F32),
        "inv_std": vmem((2, ndp, 1), F32),
        "gs_own": vmem((2, ndp, width), BF16),
        "mx_own": vmem((2, ndp, width), BF16),
        "mine": vmem((nz, GROUP // 2, strip, half), F32),
        "total": vmem((2, nz, strip, half), F32),
        "x_out": vmem((nz, strip, half), BF16),
        "x_in": vmem((nz, strip, half), BF16),
        "x_sem": DMA((2,)),
        "last_out": vmem((strip, half), F32),
        "last_in": vmem((strip, half), F32),
        "last_sem": DMA((2,)),
    }

    def both_ways(name, shape, count):
        scratch[name + "_out"] = vmem(shape, BF16)
        scratch[name + "_in"] = vmem(shape, BF16)
        scratch[name + "_ss"] = DMA((count,))
        scratch[name + "_rs"] = DMA((count,))

    for prefix in "ab":
        for c in "01":
            both_ways(prefix + "z" + c, (nz, GROUP, width), nz)
            both_ways(prefix + "j" + c, (GROUP, nz, width), GROUP)
    for name in ("fr", "gs", "mx"):
        both_ways(name, (2, ndp, width), 2)
    both_ways("sib", (nz, GROUP // 2, strip, half), nz // 2)
    both_ways("y1", (2, nz, strip, half), 2)
    both_ways("y2", (4, nz, strip, half), 4)
    both_ways("zr", (nz, strip, half), nz)

    in_vmem = pl.BlockSpec(memory_space=pltpu.VMEM)
    anywhere = pl.BlockSpec(memory_space=pl.ANY)
    mixed, grad_source, grad_out = pl.pallas_call(
        functools.partial(kernel, ndp, list(inputs) + list(outputs) + list(scratch)),
        out_shape=list(outputs.values()),
        in_specs=[anywhere if name.startswith("weight") else in_vmem for name in inputs],
        out_specs=[in_vmem] * 3,
        scratch_shapes=list(scratch.values()),
        compiler_params=pltpu.CompilerParams(
            collective_id=1, has_side_effects=True, vmem_limit_bytes=60 * 1024 * 1024
        ),
        name="module",
    )(*inputs.values())
    return (mixed, grad_source, grad_out.T)


def solution(mesh):
    return jax.shard_map(
        local,
        mesh=mesh,
        in_specs=(
            P(("dp", "tensor"), None),
            P(("dp", "tensor"), None),
            P(("dp", "tensor")),
            P(),
            P(None, "tensor"),
            P("tensor", None),
            P(("dp", "tensor"), None),
        ),
        out_specs=(P(("dp", "tensor"), None), P(("dp", "tensor"), None), P("tensor", "dp")),
        check_vma=False,
    )
```

time: 703 us -> 120 us (0.17)
  blocking collectives: 390 us -> 0 us
  starting transfers between devices: 118 us -> 0 us
  Pallas kernels: 0 us -> 112 us
  waiting for transfers between devices: 87.7 us -> 0 us
  matrix products: 34.5 us -> 0 us
  local copies, waits for them, and re-layouts: 39.5 us -> 6.66 us
  between operations: 16.1 us -> 1.29 us
  other arithmetic: 14 us -> 0 us
    unnamed x1 -> x0, blocking collectives: 334 us -> none
    pallas_call x0 -> x1, Pallas kernels: none -> 112 us  [local(): pl.pallas_call(functools.partial(kernel, ndp, list(inputs) + list(outputs...]
    unnamed x32 -> x0, starting transfers between devices: 105 us -> none
    all_to_all x2 -> x0, blocking collectives: 55.7 us -> none  [the longest x1 38.6 us: local(): lax.all_to_all(outgoing, 'dp', split_axis=0, concat_axis=0, tiled=True)]
    reduce_scatter x2 -> x0, waiting for transfers between devices: 49.5 us -> none  [the longest x1 33.1 us: local(): lax.psum_scatter(jnp.dot(piece, weight_out, preferred_element_type=jnp.fl...]
    all_gather x2 -> x0, waiting for transfers between devices: 37.8 us -> none  [the longest x1 27.4 us: local(): grad_all = lax.all_gather(grad_rows, 'tensor', axis=0, tiled=True)]
    dot_general x4 -> x0, matrix products: 34.5 us -> none  [the longest x1 11.6 us: local(): jnp.dot(piece, weight_in.T, preferred_element_type=jnp.float32)]
    unnamed x68 -> x3, local copies, waits for them, and re-layouts: 32.7 us -> 5.37 us
  transfers between devices with their start and end apart: 37 -> 0, of which waited for: 5 -> 0; matrix products, arithmetic and copies ran while one was open for 56% -> 0% of each run, Pallas kernels for 0% -> 0%
where the time goes in v2:
time: 120 us; the launch traced here: 119 us
  Pallas kernels  112 us (93%)
  local copies, waits for them, and re-layouts  6.66 us (6%)
  between operations  1.29 us (1%)
    pallas_call x1, Pallas kernels, local(): pl.pallas_call(functools.partial(kernel, ndp, list(inputs) + list(outputs...  112 us
    unnamed x3, local copies, waits for them, and re-layouts  5.37 us

profile of v2, /device:TPU:1, one launch (start us, length us, event | category | flops | bytes accessed | tf_op | source)
XLA Modules:
  0.0 119.5 jit_solution(3953226520759803951)
XLA Ops:
  1.3 1.3 %reshape.17.refs_3_ = f32[1,1536]{1,0:T(1,128)} reshape(f32[1536]{0:T(1024)} %param.10) | data formatting | bytes 12288 | tf_op jit(solution)/shard_map/reshape | solution.py:377
  2.6 111.5 %module.1 = (bf16[256,1536]{1,0:T(8,128)(2,1)}, bf16[128,1536]{1,0:T(8,128)(2,1)}, f32[12,1536]{1,0:T(8,128)}) custom-call(bf16[128,1536]{1,0:T(8,128)(2,1)} %refs_0_.1, s32[1,128]{1,0:T(1,128)} %bitcast.5, s32[1,1]{1,0:T(1,128)} %bitcast.3.refs_2_, f32[1,1536]{1,0:T(1,128)} %reshape.17.refs_3_, bf16[256,1536]{1,0:T(8,128)(2,1)} %refs_4_.1, ...), custom_call_target="tpu_custom_call" | custom-call | tf_op jit(solution)/shard_map/module/pallas_call | solution.py:431
  114.1 2.1 %copy.14 = bf16[256,1536]{1,0:T(8,128)(2,1)} copy(bf16[256,1536]{1,0:T(8,128)(2,1)} %get-tuple-element.12) | data formatting | bytes 1572864
  116.2 1.8 %copy.15 = bf16[128,1536]{1,0:T(8,128)(2,1)} copy(bf16[128,1536]{1,0:T(8,128)(2,1)} %get-tuple-element.13) | data formatting | bytes 786432
  117.9 1.5 %copy.16 = f32[1536,12]{0,1:T(8,128)} copy(f32[1536,12]{0,1:T(8,128)} %bitcast.4) | data formatting | bytes 147456

commit v3 on v2

v3 whole, which is shorter than its diff:
```python
import functools
from types import SimpleNamespace

import jax
import jax.numpy as jnp
from jax import lax
from jax.experimental import pallas as pl
from jax.experimental.pallas import tpu as pltpu
from jax.sharding import PartitionSpec as P

epsilon = 1e-05
ABSENT = 64.0
MESH = pl.DeviceIdType.MESH
GROUP = 16
RING = 4
DMA = pltpu.SemaphoreType.DMA
BF16, F32 = jnp.bfloat16, jnp.float32


def remote(src, dst, send_sem, recv_sem, device):
    return pltpu.make_async_remote_copy(
        src_ref=src, dst_ref=dst, send_sem=send_sem, recv_sem=recv_sem, device_id=device, device_id_type=MESH
    )


class Exchange:
    def __init__(self, n, place, device_of, buffers):
        self.n, self.place, self.device_of = n, place, device_of
        self.src, self.dst, self.send_sem, self.recv_sem = buffers

    def _out(self, offset):
        p = lax.rem(self.place + offset, self.n)
        return remote(
            self.src.at[p], self.dst.at[self.place], self.send_sem.at[p], self.recv_sem.at[self.place], self.device_of(p)
        )

    def start(self):
        @pl.loop(1, self.n)
        def _(offset):
            self._out(offset).start()

        self.dst[self.place] = self.src[self.place]

    def wait_recv(self):
        @pl.loop(1, self.n)
        def _(offset):
            p = lax.rem(self.place + offset, self.n)
            remote(
                self.src.at[p], self.dst.at[p], self.send_sem.at[p], self.recv_sem.at[p], self.device_of(p)
            ).wait_recv()

    def wait_send(self):
        @pl.loop(1, self.n)
        def _(offset):
            self._out(offset).wait_send()


def picking(source, n):
    return (lax.broadcasted_iota(jnp.int32, (source.shape[0], n), 1) == source).astype(F32).astype(BF16)


def swap_rows(outer, inner, rows):
    n = outer * inner
    row = lax.broadcasted_iota(jnp.int32, (n, 1), 0)
    matrix = picking(lax.rem(row, outer) * inner + row // outer, n)
    return jnp.dot(matrix, rows, preferred_element_type=F32).astype(BF16)


def slot_matrix(routes_ref, live_ref, ndp, capacity):
    count = routes_ref.shape[1]
    row = lax.broadcasted_iota(jnp.int32, (count, count), 0)
    col = lax.broadcasted_iota(jnp.int32, (count, count), 1)
    target = routes_ref[...]
    wide = jnp.broadcast_to(target, (count, count))
    tall = jnp.sum(jnp.where(row == col, wide, 0), axis=1, keepdims=True)
    rank = jnp.sum(((tall == wide) & (row < col)).astype(jnp.int32), axis=0, keepdims=True)
    alive = lax.broadcasted_iota(jnp.int32, (1, count), 1) < live_ref[...]
    slot = jnp.where(alive, rank * ndp + target, -1)
    return (lax.broadcasted_iota(jnp.int32, (ndp * capacity, count), 0) == slot).astype(F32)


def dot_t(left, right):
    return lax.dot_general(left, right, (((1,), (1,)), ((), ())), preferred_element_type=F32)


def t_dot(left, right):
    return lax.dot_general(left, right, (((0,), (0,)), ((), ())), preferred_element_type=F32)


def tiles(total, size, body, start=0):
    @pl.loop(0, total // size)
    def _(i):
        body(pl.ds(pl.multiple_of(start + i * size, size), size))


class Route:
    def __init__(self, z_first, over_z, over_j):
        self.z_first = z_first
        self.nz, self.nj = over_z.n, over_j.n
        self.first, self.second = (over_z, over_j) if z_first else (over_j, over_z)

    def _send(self, exchange, rows):
        exchange.src[...] = rows.reshape(exchange.src.shape)
        exchange.start()

    def _got(self, exchange):
        exchange.wait_recv()
        shape = exchange.dst.shape
        return exchange.dst[...].reshape(shape[0] * shape[1], shape[2])

    def start(self, rows):
        self._send(self.first, rows if self.z_first else swap_rows(self.nz, self.nj, rows))

    def middle(self):
        a, b = (self.nz, self.nj) if self.z_first else (self.nj, self.nz)
        self._send(self.second, swap_rows(a, b, self._got(self.first)))

    def finish(self):
        rows = self._got(self.second)
        return swap_rows(self.nj, self.nz, rows) if self.z_first else rows

    def wait_send(self):
        self.first.wait_send()
        self.second.wait_send()


def kernel(ndp, names, *refs):
    r = SimpleNamespace(**dict(zip(names, refs)))
    me, t = lax.axis_index("dp"), lax.axis_index("tensor")
    nz = ndp // GROUP
    z, j = me // GROUP, lax.rem(me, GROUP)
    y, xl, core = j // 4, lax.rem(j // 2, 2), lax.rem(j, 2)
    z_device = lambda p: {"dp": p * GROUP + j}
    j_device = lambda p: {"dp": z * GROUP + p}
    y_device = lambda p: {"dp": z * GROUP + p * 4 + xl * 2 + core}
    x_device = {"dp": me + 2 - 4 * xl}
    sibling = {"dp": me + 1 - 2 * core}
    partner = {"dp": me + 2 - 4 * xl, "tensor": 1 - t}
    width = r.source.shape[1]
    units = r.win.shape[1]
    half = units // 2
    wide = width // 2
    halves = [slice(0, wide), slice(wide, width)]

    load_cot = pltpu.make_async_copy(r.cotangent, r.cot, r.load_sem.at[2])
    load_in = pltpu.make_async_copy(r.weight_in, r.win, r.load_sem.at[0])
    load_out = pltpu.make_async_copy(r.weight_out, r.wout, r.load_sem.at[1])
    load_cot.start()
    load_in.start()
    load_out.start()

    barrier = pltpu.get_barrier_semaphore()

    @pl.loop(1, nz)
    def _(offset):
        pl.semaphore_signal(barrier, inc=1, device_id=z_device(lax.rem(z + offset, nz)), device_id_type=MESH)

    @pl.loop(1, GROUP)
    def _(offset):
        pl.semaphore_signal(barrier, inc=1, device_id=j_device(lax.rem(j + offset, GROUP)), device_id_type=MESH)

    pl.semaphore_signal(barrier, inc=1, device_id=partner, device_id_type=MESH)

    def exchange(name, n, place, device_of):
        return Exchange(n, place, device_of, tuple(getattr(r, name + end) for end in ("_out", "_in", "_ss", "_rs")))

    def routed(name, z_first):
        return Route(z_first, exchange(name + "z", nz, z, z_device), exchange(name + "j", GROUP, j, j_device))

    def one_way(name, slot, device, part=None):
        out, land, ss, rs = (getattr(r, name + end) for end in ("_out", "_in", "_ss", "_rs"))
        index, sem = (slot, slot) if part is None else ((slot, slice(None), halves[part]), 2 * slot + part)
        return remote(out.at[index], land.at[index], ss.at[sem], rs.at[sem], device)

    r.gain_row[...] = r.gain[...].reshape(1, -1)
    hot = slot_matrix(r.routes, r.live, ndp, 2)
    r.hot[...] = hot.astype(BF16)
    first = lax.broadcasted_iota(jnp.int32, (ndp, width), 1) == 0

    def outgoing(rank):
        part = hot[rank * ndp : (rank + 1) * ndp]
        empty = jnp.sum(part, axis=1, keepdims=True) < 0.5
        rows = jnp.dot(part.astype(BF16), r.source[...], preferred_element_type=F32)
        return jnp.where(empty & first, ABSENT, rows).astype(BF16)

    there = [routed("a" + str(i), i == 0) for i in range(4)]
    leaving = outgoing(0)
    pl.semaphore_wait(barrier, nz + GROUP - 1)
    there[0].start(leaving[:, halves[0]])
    there[1].start(leaving[:, halves[1]])
    load_cot.wait()
    cot_copy = remote(r.cot, r.cot_in, r.cot_sem.at[0], r.cot_sem.at[1], partner)
    cot_copy.start()
    leaving = outgoing(1)
    there[2].start(leaving[:, halves[0]])
    there[3].start(leaving[:, halves[1]])

    strip = width // (nz * 8)
    step = width // RING

    def turn(side, rows):
        @pl.loop(0, RING)
        def _(i):
            row = lax.broadcasted_iota(jnp.int32, (step, 1), 0)
            x_at, z_at, rest = row // (step // 2), lax.rem(row // strip, nz), lax.rem(row, strip)
            pick = picking((z_at * 8 + i * 2 + x_at) * strip + rest, width)
            at = pl.ds(pl.multiple_of(i * step, step), step)
            r.turned[at, side * 2 * ndp : (side + 1) * 2 * ndp] = dot_t(pick, rows).astype(BF16)

    def order_cot(side, rows):
        rows = swap_rows(ndp, 2, rows)
        r.cots[side * 2 * ndp : (side + 1) * 2 * ndp] = rows
        turn(side, rows)

    order_cot(0, r.cot[...])
    there[1].middle()
    there[0].middle()
    load_in.wait()
    load_out.wait()

    def process(k):
        c = k % 2
        rows = pl.ds(k * ndp, ndp)
        slots = (r.fr_out if k < 2 else r.fr_in)[c].astype(F32)
        present = slots[:, :1] < 0.5 * ABSENT
        frames = jnp.where(present, slots, 0.0)
        centred = frames - jnp.mean(frames, axis=1, keepdims=True)
        inv_std = lax.rsqrt(jnp.mean(centred * centred, axis=1, keepdims=True) + epsilon)
        normed = centred * inv_std
        if k < 2:
            r.normed[c] = normed
            r.inv_std[c] = inv_std
        r.scaled[...] = (normed * r.gain_row[...]).astype(BF16)
        r.grads[rows] = jnp.where(present, r.cots[rows].astype(F32), 0.0).astype(BF16)

        def tile(n):
            hidden = jnp.dot(r.scaled[...], r.win[:, n], preferred_element_type=F32)
            grad_act = 0.5 * dot_t(r.grads[rows], r.wout[n, :])
            gate = jax.nn.sigmoid(hidden)
            r.act[rows, n] = jnp.where(present, hidden * gate, 0.0).astype(BF16)
            r.gh[rows, n] = (grad_act * gate * (1.0 + hidden * (1.0 - gate))).astype(BF16)

        tiles(units, 512, tile)

    def scaled_grad(k, out, c, start=0, length=None):
        def tile(n):
            out[c, :, n] = dot_t(r.gh[pl.ds(k * ndp, ndp), :], r.win[n, :]).astype(BF16)

        tiles(length or width, 384, tile, start)

    def mix(k, out, c):
        def tile(n):
            out[c, :, n] = jnp.dot(
                r.act[pl.ds(k * ndp, ndp), :], r.wout[:, n], preferred_element_type=F32
            ).astype(BF16)

        tiles(width, 512, tile)

    frames_over = [one_way("fr", i // 2, partner, i % 2) for i in range(4)]

    def land(i):
        r.fr_out[i // 2, :, halves[i % 2]] = there[i].finish()
        frames_over[i].start()

    there[2].middle()
    land(0)
    land(1)
    there[3].middle()
    process(0)
    scaled_grad(0, r.gs_own, 0)
    cot_copy.wait_recv()
    order_cot(1, r.cot_in[...])
    land(2)
    land(3)
    frames_over[0].wait_recv()
    frames_over[1].wait_recv()
    process(2)
    sums = [one_way("gs", i // 2, partner, i % 2) for i in range(4)]

    def send_sums(c):
        for part in range(2):
            scaled_grad(2 + c, r.gs_out, c, part * wide, wide)
            sums[2 * c + part].start()

    send_sums(0)
    process(1)
    scaled_grad(1, r.gs_own, 1)
    frames_over[2].wait_recv()
    frames_over[3].wait_recv()
    process(3)
    send_sums(1)

    up, down, opposite = lax.rem(y + 1, RING), lax.rem(y + 3, RING), lax.rem(y + 2, RING)
    order = [opposite, up, down, y]

    def product(y_at, which):
        columns = pl.ds(pl.multiple_of(which * half, half), half)
        left = r.turned[pl.ds(pl.multiple_of(y_at * step, step), step), :]
        return (0.5 * jnp.dot(left, r.act[:, columns], preferred_element_type=F32)).reshape(2, step // 2, half)

    def to_sibling(i):
        part = pl.ds(2 * order[i], 2)
        return remote(r.sib_out.at[part], r.sib_in.at[part], r.sib_ss.at[i], r.sib_rs.at[i], sibling)

    for i in range(4):
        r.sib_out[pl.ds(2 * order[i], 2)] = product(order[i], 1 - core).astype(BF16)
        to_sibling(i).start()

    def keep(i):
        r.mine[pl.ds(2 * order[i], 2)] = product(order[i], core)
        to_sibling(i).wait_recv()

    block = half // 2
    blocks = [slice(0, block), slice(block, half)]
    part_rows = step // 4

    def cores(y_at, x_at, b):
        p = y_at * 2 + x_at
        return r.mine[p, :, blocks[b]] + r.sib_in[p, :, blocks[b]].astype(F32)

    def ring1(name, slot):
        return one_way(name, slot, y_device(down) if slot else y_device(up))

    def ring2(name, slot):
        return one_way(name, slot, y_device(down) if slot // 2 else y_device(up))

    def send(copy, buffer, index, value):
        buffer[index] = value.astype(BF16)
        copy.start()

    def x_first(i):
        return remote(r.bx_out.at[i], r.bx_in.at[i], r.bx_ss.at[i], r.bx_rs.at[i], x_device)

    keep(0)
    for s in range(2):
        send(ring1("a1", s), r.a1_out, s, cores(opposite, s, 0))
    send(x_first(0), r.bx_out, 0, cores(opposite, 1 - xl, 1))
    keep(1)
    send(ring2("a2", 1), r.a2_out, 1, cores(up, 1, 0))
    send(x_first(1), r.bx_out, 1, cores(up, 1 - xl, 1))
    keep(2)
    send(ring2("a2", 2), r.a2_out, 2, cores(down, 0, 0))
    send(x_first(2), r.bx_out, 2, cores(down, 1 - xl, 1))
    keep(3)
    send(x_first(3), r.bx_out, 3, cores(y, 1 - xl, 1))

    def gradient(c):
        normed = r.normed[c]
        g = (r.gs_own[c].astype(F32) + r.gs_in[c].astype(F32)) * r.gain_row[...]
        first_mean = jnp.mean(g, axis=1, keepdims=True)
        second_mean = jnp.mean(g * normed, axis=1, keepdims=True)
        own = r.grads[pl.ds(c * ndp, ndp)].astype(F32)
        return (own + r.inv_std[c] * (g - first_mean - normed * second_mean)).astype(BF16)

    back = [routed("b" + str(i), i % 2 == 0) for i in range(4)]

    def give(c):
        sums[2 * c].wait_recv()
        sums[2 * c + 1].wait_recv()
        rows = gradient(c)
        back[2 * c].start(rows[:, halves[0]])
        back[2 * c + 1].start(rows[:, halves[1]])

    give(0)
    mix(2, r.mx_out, 0)
    mix(3, r.mx_out, 1)
    ring1("a1", 0).wait_recv()
    send(ring2("a2", 0), r.a2_out, 0, cores(up, 0, 0) + r.a1_in[0].astype(F32))
    ring1("a1", 1).wait_recv()
    send(ring2("a2", 3), r.a2_out, 3, cores(down, 1, 0) + r.a1_in[1].astype(F32))

    def summed(i):
        r.bsum[i] = cores(order[i], xl, 1) + r.bx_in[i].astype(F32)

    x_first(0).wait_recv()
    summed(0)
    for s in range(2):
        send(ring1("b1", s), r.b1_out, s, r.bsum[0, s * part_rows : (s + 1) * part_rows])
    back[1].middle()
    x_first(1).wait_recv()
    summed(1)
    send(ring2("b2", 1), r.b2_out, 1, r.bsum[1, part_rows:])
    x_first(2).wait_recv()
    summed(2)
    send(ring2("b2", 2), r.b2_out, 2, r.bsum[2, :part_rows])
    give(1)
    mixes = [one_way("mx", c, partner) for c in range(2)]
    mixes[0].start()
    mixes[1].start()
    back[0].middle()
    ring1("b1", 0).wait_recv()
    send(ring2("b2", 0), r.b2_out, 0, r.bsum[1, :part_rows] + r.b1_in[0].astype(F32))
    ring1("b1", 1).wait_recv()
    send(ring2("b2", 3), r.b2_out, 3, r.bsum[2, part_rows:] + r.b1_in[1].astype(F32))
    mix(0, r.mx_own, 0)
    mix(1, r.mx_own, 1)
    for slot in range(4):
        ring2("a2", slot).wait_recv()
    for s in range(2):
        r.total[s] = cores(y, s, 0) + r.a2_in[s].astype(F32) + r.a2_in[2 + s].astype(F32)
    r.ax_out[...] = r.total[1 - xl].astype(BF16)
    x_last = remote(r.ax_out, r.ax_in, r.ax_ss.at[0], r.ax_rs.at[0], x_device)
    x_last.start()
    back[3].middle()
    back[2].middle()
    x_first(3).wait_recv()
    summed(3)
    for slot in range(4):
        ring2("b2", slot).wait_recv()
    over_z = [exchange("s" + str(b), nz, z, z_device) for b in range(2)]
    for s in range(2):
        at = slice(s * part_rows, (s + 1) * part_rows)
        r.bsum[3, at] = r.bsum[3, at] + r.b2_in[s].astype(F32) + r.b2_in[2 + s].astype(F32)
    r.s1_out[...] = r.bsum[3].astype(BF16).reshape(r.s1_out.shape)
    over_z[1].start()
    x_last.wait_recv()
    r.s0_out[...] = (r.total[xl] + r.ax_in[...].astype(F32)).astype(BF16).reshape(r.s0_out.shape)
    over_z[0].start()

    r.rows[0, :, halves[0]] = back[0].finish()
    r.rows[0, :, halves[1]] = back[1].finish()
    for c in range(2):
        mixes[c].wait_recv()
    mixed_rows = []
    for c in range(2):
        slots = r.fr_out[c].astype(F32)
        frames = jnp.where(slots[:, :1] < 0.5 * ABSENT, slots, 0.0)
        mixed_rows.append((frames + 0.5 * (r.mx_own[c].astype(F32) + r.mx_in[c].astype(F32))).astype(BF16))
    r.mixed[...] = swap_rows(2, ndp, jnp.concatenate(mixed_rows, axis=0))
    for b in (1, 0):
        over_z[b].wait_recv()
        r.last_out[:, blocks[b]] = jnp.sum((r.s0_in, r.s1_in)[b][...].astype(F32), axis=0)
    last = remote(r.last_out, r.last_in, r.last_sem.at[0], r.last_sem.at[1], sibling)
    last.start()
    r.rows[1, :, halves[1]] = back[3].finish()
    r.rows[1, :, halves[0]] = back[2].finish()
    r.grad_source[...] = (t_dot(r.hot[:ndp], r.rows[0]) + t_dot(r.hot[ndp:], r.rows[1])).astype(BF16)

    last.wait_recv()
    own, other = r.last_out[...], r.last_in[...]
    count = own.shape[0] // 2
    is_low = core == 0
    own = jnp.where(is_low, own[:count], own[count:])
    other = jnp.where(is_low, other[:count], other[count:])
    r.grad_out[:, :half] = jnp.where(is_low, own, other)
    r.grad_out[:, half:] = jnp.where(is_low, other, own)

    last.wait_send()
    cot_copy.wait_send()
    x_last.wait_send()
    for copy in sums + mixes + frames_over + there + back + over_z:
        copy.wait_send()
    for name in ("a", "b"):
        for slot in range(2):
            ring1(name + "1", slot).wait_send()
        for slot in range(4):
            ring2(name + "2", slot).wait_send()
    for i in range(4):
        to_sibling(i).wait_send()
        x_first(i).wait_send()


def finish_kernel(mixed, grad_source, grad_out, mixed_out, grad_source_out, grad_out_out):
    mixed_out[...] = mixed[...]
    grad_source_out[...] = grad_source[...]
    grad_out_out[...] = grad_out[...]


def local(source_frames, routes, live_frames, norm_gain, weight_in, weight_out, cotangent):
    ndp = lax.axis_size("dp")
    nz = ndp // GROUP
    width, units = weight_in.shape
    half, strip = units // 2, width // ndp * 2
    block, tall = half // 2, width // 8
    vmem = pltpu.VMEM
    inputs = {
        "source": source_frames,
        "routes": routes.reshape(1, -1),
        "live": live_frames.reshape(1, 1),
        "gain": norm_gain,
        "cotangent": cotangent,
        "weight_in": weight_in,
        "weight_out": weight_out,
    }
    outputs = {
        "mixed": jax.ShapeDtypeStruct(cotangent.shape, BF16),
        "grad_source": jax.ShapeDtypeStruct(source_frames.shape, BF16),
        "grad_out": jax.ShapeDtypeStruct((width // ndp, units), F32),
    }
    scratch = {
        "win": vmem(weight_in.shape, BF16),
        "wout": vmem(weight_out.shape, BF16),
        "cot": vmem(cotangent.shape, BF16),
        "cot_in": vmem(cotangent.shape, BF16),
        "cot_sem": DMA((2,)),
        "cots": vmem((4 * ndp, width), BF16),
        "load_sem": DMA((3,)),
        "hot": vmem((2 * ndp, source_frames.shape[0]), BF16),
        "turned": vmem((width, 4 * ndp), BF16),
        "grads": vmem((4 * ndp, width), BF16),
        "act": vmem((4 * ndp, units), BF16),
        "gh": vmem((4 * ndp, units), BF16),
        "gain_row": vmem((1, width), F32),
        "scaled": vmem((ndp, width), BF16),
        "normed": vmem((2, ndp, width), F32),
        "inv_std": vmem((2, ndp, 1), F32),
        "gs_own": vmem((2, ndp, width), BF16),
        "mx_own": vmem((2, ndp, width), BF16),
        "rows": vmem((2, ndp, width), BF16),
        "mine": vmem((8, tall, half), F32),
        "total": vmem((2, tall, block), F32),
        "bsum": vmem((4, tall, block), F32),
        "last_out": vmem((strip, half), F32),
        "last_in": vmem((strip, half), F32),
        "last_sem": DMA((2,)),
    }

    def both_ways(name, shape, count):
        scratch[name + "_out"] = vmem(shape, BF16)
        scratch[name + "_in"] = vmem(shape, BF16)
        scratch[name + "_ss"] = DMA((count,))
        scratch[name + "_rs"] = DMA((count,))

    for prefix in "ab":
        for i in "0123":
            both_ways(prefix + i + "z", (nz, GROUP, width // 2), nz)
            both_ways(prefix + i + "j", (GROUP, nz, width // 2), GROUP)
    for name, count in (("fr", 4), ("gs", 4), ("mx", 2)):
        both_ways(name, (2, ndp, width), count)
    both_ways("sib", (8, tall, half), 4)
    both_ways("a1", (2, tall, block), 2)
    both_ways("a2", (4, tall, block), 4)
    both_ways("b1", (2, tall // 2, block), 2)
    both_ways("b2", (4, tall // 2, block), 4)
    both_ways("ax", (tall, block), 1)
    both_ways("bx", (4, tall, block), 4)
    both_ways("s0", (nz, strip, block), nz)
    both_ways("s1", (nz, strip, block), nz)

    in_vmem = pl.BlockSpec(memory_space=pltpu.VMEM)
    anywhere = pl.BlockSpec(memory_space=pl.ANY)
    from_hbm = ("weight_in", "weight_out", "cotangent")
    results = pl.pallas_call(
        functools.partial(kernel, ndp, list(inputs) + list(outputs) + list(scratch)),
        out_shape=list(outputs.values()),
        in_specs=[anywhere if name in from_hbm else in_vmem for name in inputs],
        out_specs=[in_vmem] * 3,
        scratch_shapes=list(scratch.values()),
        compiler_params=pltpu.CompilerParams(
            collective_id=1, has_side_effects=True, vmem_limit_bytes=60 * 1024 * 1024
        ),
        name="module",
    )(*inputs.values())
    mixed, grad_source, grad_out = pl.pallas_call(
        finish_kernel,
        out_shape=list(outputs.values()),
        in_specs=[in_vmem] * 3,
        out_specs=[in_vmem] * 3,
        name="finish",
    )(*results)
    return (mixed, grad_source, grad_out.T)


def solution(mesh):
    return jax.shard_map(
        local,
        mesh=mesh,
        in_specs=(
            P(("dp", "tensor"), None),
            P(("dp", "tensor"), None),
            P(("dp", "tensor")),
            P(),
            P(None, "tensor"),
            P("tensor", None),
            P(("dp", "tensor"), None),
        ),
        out_specs=(P(("dp", "tensor"), None), P(("dp", "tensor"), None), P("tensor", "dp")),
        check_vma=False,
    )
```

time: 120 us -> 110 us (0.917)
  local copies, waits for them, and re-layouts: 6.66 us -> 0 us
  Pallas kernels: 112 us -> 109 us
    unnamed x3 -> x0, local copies, waits for them, and re-layouts: 5.37 us -> none
    pallas_call x1, Pallas kernels: 112 us -> 106 us  [local(): pl.pallas_call(functools.partial(kernel, ndp, list(inputs) + list(outputs...]
    pallas_call x0 -> x1, Pallas kernels: none -> 2.31 us  [local(): pl.pallas_call(finish_kernel, out_shape=list(outputs.values()), in_specs=...]
    reshape x1 -> x0, local copies, waits for them, and re-layouts: 1.3 us -> none  [local(): norm_gain.reshape(1, -1)]
where the time goes in v3:
time: 110 us
  Pallas kernels  109 us (99%)
  between operations  1.29 us (1%)
    pallas_call x1, Pallas kernels, local(): pl.pallas_call(functools.partial(kernel, ndp, list(inputs) + list(outputs...  106 us
    pallas_call x1, Pallas kernels, local(): pl.pallas_call(finish_kernel, out_shape=list(outputs.values()), in_specs=...  2.31 us

profile of v3, /device:TPU:1, one launch (start us, length us, event | category | flops | bytes accessed | tf_op | source)
XLA Modules:
  0.0 110.1 jit_solution(17097100873115366923)
XLA Ops:
  1.3 106.5 %module.1 = (bf16[256,1536]{1,0:T(8,128)(2,1)}, bf16[128,1536]{1,0:T(8,128)(2,1)}, f32[12,1536]{1,0:T(8,128)}) custom-call(bf16[128,1536]{1,0:T(8,128)(2,1)} %refs_0_.1, s32[1,128]{1,0:T(1,128)} %bitcast.4, s32[1,1]{1,0:T(1,128)} %bitcast.3.refs_2_, f32[1536]{0:T(1024)} %refs_3_.1, bf16[256,1536]{1,0:T(8,128)(2,1)} %refs_4_.1, bf16[1536,1536]{1,0:T(8,128)(2,1)} %refs_5_.1, ...), custom_call_target="tpu_custom_call" | custom-call | tf_op jit(solution)/shard_map/module/pallas_call | solution.py:543
  107.8 2.3 %finish.1 = (bf16[256,1536]{1,0:T(8,128)(2,1)}, bf16[128,1536]{1,0:T(8,128)(2,1)}, f32[12,1536]{1,0:T(8,128)}) custom-call(bf16[256,1536]{1,0:T(8,128)(2,1)} %get-tuple-element.9.mixed, bf16[128,1536]{1,0:T(8,128)(2,1)} %get-tuple-element.10.grad_source, f32[12,1536]{1,0:T(8,128)} %get-tuple-element.11.grad_out), custom_call_target="tpu_custom_call" | custom-call | tf_op jit(solution)/shard_map/finish/pallas_call | solution.py:554

commit v4 on v3

--- a/solution.py
+++ b/solution.py
@@ -28,31 +28,26 @@
         self.n, self.place, self.device_of = n, place, device_of
         self.src, self.dst, self.send_sem, self.recv_sem = buffers
 
-    def _out(self, offset):
-        p = lax.rem(self.place + offset, self.n)
-        return remote(
-            self.src.at[p], self.dst.at[self.place], self.send_sem.at[p], self.recv_sem.at[self.place], self.device_of(p)
-        )
-
     def start(self):
         @pl.loop(1, self.n)
         def _(offset):
-            self._out(offset).start()
+            p = (self.place + offset) & (self.n - 1)
+            remote(
+                self.src.at[p], self.dst.at[self.place], self.send_sem.at[0], self.recv_sem.at[0], self.device_of(p)
+            ).start()
 
         self.dst[self.place] = self.src[self.place]
 
+    def _all(self):
+        part = pl.ds(0, self.n - 1)
+        p = (self.place + 1) & (self.n - 1)
+        return remote(self.src.at[part], self.dst.at[part], self.send_sem.at[0], self.recv_sem.at[0], self.device_of(p))
+
     def wait_recv(self):
-        @pl.loop(1, self.n)
-        def _(offset):
-            p = lax.rem(self.place + offset, self.n)
-            remote(
-                self.src.at[p], self.dst.at[p], self.send_sem.at[p], self.recv_sem.at[p], self.device_of(p)
-            ).wait_recv()
+        self._all().wait_recv()
 
     def wait_send(self):
-        @pl.loop(1, self.n)
-        def _(offset):
-            self._out(offset).wait_send()
+        self._all().wait_send()
 
 
 def picking(source, n):
@@ -183,7 +178,7 @@
         rows = jnp.dot(part.astype(BF16), r.source[...], preferred_element_type=F32)
         return jnp.where(empty & first, ABSENT, rows).astype(BF16)
 
-    there = [routed("a" + str(i), i == 0) for i in range(4)]
+    there = [routed("a" + str(i), i < 2) for i in range(4)]
     leaving = outgoing(0)
     pl.semaphore_wait(barrier, nz + GROUP - 1)
     there[0].start(leaving[:, halves[0]])
@@ -213,8 +208,8 @@
         turn(side, rows)
 
     order_cot(0, r.cot[...])
-    there[1].middle()
     there[0].middle()
+    there[2].middle()
     load_in.wait()
     load_out.wait()
 
@@ -262,16 +257,17 @@
         r.fr_out[i // 2, :, halves[i % 2]] = there[i].finish()
         frames_over[i].start()
 
-    there[2].middle()
+    there[1].middle()
     land(0)
+    there[3].middle()
     land(1)
-    there[3].middle()
     process(0)
     scaled_grad(0, r.gs_own, 0)
     cot_copy.wait_recv()
     order_cot(1, r.cot_in[...])
     land(2)
     land(3)
+    mix(0, r.mx_own, 0)
     frames_over[0].wait_recv()
     frames_over[1].wait_recv()
     process(2)
@@ -285,6 +281,8 @@
     send_sums(0)
     process(1)
     scaled_grad(1, r.gs_own, 1)
+    for route in there:
+        route.wait_send()
     frames_over[2].wait_recv()
     frames_over[3].wait_recv()
     process(3)
@@ -332,15 +330,15 @@
         return remote(r.bx_out.at[i], r.bx_in.at[i], r.bx_ss.at[i], r.bx_rs.at[i], x_device)
 
     keep(0)
+    send(x_first(0), r.bx_out, 0, cores(opposite, 1 - xl, 1))
     for s in range(2):
         send(ring1("a1", s), r.a1_out, s, cores(opposite, s, 0))
-    send(x_first(0), r.bx_out, 0, cores(opposite, 1 - xl, 1))
     keep(1)
+    send(x_first(1), r.bx_out, 1, cores(up, 1 - xl, 1))
     send(ring2("a2", 1), r.a2_out, 1, cores(up, 1, 0))
-    send(x_first(1), r.bx_out, 1, cores(up, 1 - xl, 1))
     keep(2)
+    send(x_first(2), r.bx_out, 2, cores(down, 1 - xl, 1))
     send(ring2("a2", 2), r.a2_out, 2, cores(down, 0, 0))
-    send(x_first(2), r.bx_out, 2, cores(down, 1 - xl, 1))
     keep(3)
     send(x_first(3), r.bx_out, 3, cores(y, 1 - xl, 1))
 
@@ -352,7 +350,7 @@
         own = r.grads[pl.ds(c * ndp, ndp)].astype(F32)
         return (own + r.inv_std[c] * (g - first_mean - normed * second_mean)).astype(BF16)
 
-    back = [routed("b" + str(i), i % 2 == 0) for i in range(4)]
+    back = [routed("b" + str(i), i < 2) for i in range(4)]
 
     def give(c):
         sums[2 * c].wait_recv()
@@ -362,8 +360,6 @@
         back[2 * c + 1].start(rows[:, halves[1]])
 
     give(0)
-    mix(2, r.mx_out, 0)
-    mix(3, r.mx_out, 1)
     ring1("a1", 0).wait_recv()
     send(ring2("a2", 0), r.a2_out, 0, cores(up, 0, 0) + r.a1_in[0].astype(F32))
     ring1("a1", 1).wait_recv()
@@ -376,7 +372,7 @@
     summed(0)
     for s in range(2):
         send(ring1("b1", s), r.b1_out, s, r.bsum[0, s * part_rows : (s + 1) * part_rows])
-    back[1].middle()
+    back[0].middle()
     x_first(1).wait_recv()
     summed(1)
     send(ring2("b2", 1), r.b2_out, 1, r.bsum[1, part_rows:])
@@ -385,15 +381,16 @@
     send(ring2("b2", 2), r.b2_out, 2, r.bsum[2, :part_rows])
     give(1)
     mixes = [one_way("mx", c, partner) for c in range(2)]
+    mix(2, r.mx_out, 0)
     mixes[0].start()
-    mixes[1].start()
-    back[0].middle()
+    back[1].middle()
     ring1("b1", 0).wait_recv()
     send(ring2("b2", 0), r.b2_out, 0, r.bsum[1, :part_rows] + r.b1_in[0].astype(F32))
     ring1("b1", 1).wait_recv()
     send(ring2("b2", 3), r.b2_out, 3, r.bsum[2, part_rows:] + r.b1_in[1].astype(F32))
-    mix(0, r.mx_own, 0)
-    mix(1, r.mx_own, 1)
+    back[2].middle()
+    mix(3, r.mx_out, 1)
+    mixes[1].start()
     for slot in range(4):
         ring2("a2", slot).wait_recv()
     for s in range(2):
@@ -402,7 +399,6 @@
     x_last = remote(r.ax_out, r.ax_in, r.ax_ss.at[0], r.ax_rs.at[0], x_device)
     x_last.start()
     back[3].middle()
-    back[2].middle()
     x_first(3).wait_recv()
     summed(3)
     for slot in range(4):
@@ -416,6 +412,7 @@
     x_last.wait_recv()
     r.s0_out[...] = (r.total[xl] + r.ax_in[...].astype(F32)).astype(BF16).reshape(r.s0_out.shape)
     over_z[0].start()
+    mix(1, r.mx_own, 1)
 
     r.rows[0, :, halves[0]] = back[0].finish()
     r.rows[0, :, halves[1]] = back[1].finish()
@@ -432,8 +429,8 @@
         r.last_out[:, blocks[b]] = jnp.sum((r.s0_in, r.s1_in)[b][...].astype(F32), axis=0)
     last = remote(r.last_out, r.last_in, r.last_sem.at[0], r.last_sem.at[1], sibling)
     last.start()
+    r.rows[1, :, halves[0]] = back[2].finish()
     r.rows[1, :, halves[1]] = back[3].finish()
-    r.rows[1, :, halves[0]] = back[2].finish()
     r.grad_source[...] = (t_dot(r.hot[:ndp], r.rows[0]) + t_dot(r.hot[ndp:], r.rows[1])).astype(BF16)
 
     last.wait_recv()
@@ -448,7 +445,7 @@
     last.wait_send()
     cot_copy.wait_send()
     x_last.wait_send()
-    for copy in sums + mixes + frames_over + there + back + over_z:
+    for copy in sums + mixes + frames_over + back + over_z:
         copy.wait_send()
     for name in ("a", "b"):
         for slot in range(2):
@@ -523,8 +520,8 @@
 
     for prefix in "ab":
         for i in "0123":
-            both_ways(prefix + i + "z", (nz, GROUP, width // 2), nz)
-            both_ways(prefix + i + "j", (GROUP, nz, width // 2), GROUP)
+            both_ways(prefix + i + "z", (nz, GROUP, width // 2), 1)
+            both_ways(prefix + i + "j", (GROUP, nz, width // 2), 1)
     for name, count in (("fr", 4), ("gs", 4), ("mx", 2)):
         both_ways(name, (2, ndp, width), count)
     both_ways("sib", (8, tall, half), 4)
@@ -534,8 +531,8 @@
     both_ways("b2", (4, tall // 2, block), 4)
     both_ways("ax", (tall, block), 1)
     both_ways("bx", (4, tall, block), 4)
-    both_ways("s0", (nz, strip, block), nz)
-    both_ways("s1", (nz, strip, block), nz)
+    both_ways("s0", (nz, strip, block), 1)
+    both_ways("s1", (nz, strip, block), 1)
 
     in_vmem = pl.BlockSpec(memory_space=pltpu.VMEM)
     anywhere = pl.BlockSpec(memory_space=pl.ANY)

time: 110 us -> 106 us (0.964)
  Pallas kernels: 109 us -> 105 us
    pallas_call x1, Pallas kernels: 106 us -> 102 us  [local(): pl.pallas_call(functools.partial(kernel, ndp, list(inputs) + list(outputs...]
where the time goes in v4:
time: 106 us
  Pallas kernels  105 us (99%)
  between operations  1.29 us (1%)
    pallas_call x1, Pallas kernels, local(): pl.pallas_call(functools.partial(kernel, ndp, list(inputs) + list(outputs...  102 us
    pallas_call x1, Pallas kernels, local(): pl.pallas_call(finish_kernel, out_shape=list(outputs.values()), in_specs=...  2.31 us

profile of v4, /device:TPU:1, one launch (start us, length us, event | category | flops | bytes accessed | tf_op | source)
XLA Modules:
  0.0 106.0 jit_solution(8806388817423432221)
XLA Ops:
  1.3 102.4 %module.1 = (bf16[256,1536]{1,0:T(8,128)(2,1)}, bf16[128,1536]{1,0:T(8,128)(2,1)}, f32[12,1536]{1,0:T(8,128)}) custom-call(bf16[128,1536]{1,0:T(8,128)(2,1)} %refs_0_.1, s32[1,128]{1,0:T(1,128)} %bitcast.4, s32[1,1]{1,0:T(1,128)} %bitcast.3.refs_2_, f32[1536]{0:T(1024)} %refs_3_.1, bf16[256,1536]{1,0:T(8,128)(2,1)} %refs_4_.1, bf16[1536,1536]{1,0:T(8,128)(2,1)} %refs_5_.1, ...), custom_call_target="tpu_custom_call" | custom-call | tf_op jit(solution)/shard_map/module/pallas_call | solution.py:540
  103.7 2.3 %finish.1 = (bf16[256,1536]{1,0:T(8,128)(2,1)}, bf16[128,1536]{1,0:T(8,128)(2,1)}, f32[12,1536]{1,0:T(8,128)}) custom-call(bf16[256,1536]{1,0:T(8,128)(2,1)} %get-tuple-element.9.mixed, bf16[128,1536]{1,0:T(8,128)(2,1)} %get-tuple-element.10.grad_source, f32[12,1536]{1,0:T(8,128)} %get-tuple-element.11.grad_out), custom_call_target="tpu_custom_call" | custom-call | tf_op jit(solution)/shard_map/finish/pallas_call | solution.py:551

commit v5 on v4

--- a/solution.py
+++ b/solution.py
@@ -258,8 +258,8 @@
         frames_over[i].start()
 
     there[1].middle()
+    there[3].middle()
     land(0)
-    there[3].middle()
     land(1)
     process(0)
     scaled_grad(0, r.gs_own, 0)
@@ -372,25 +372,20 @@
     summed(0)
     for s in range(2):
         send(ring1("b1", s), r.b1_out, s, r.bsum[0, s * part_rows : (s + 1) * part_rows])
-    back[0].middle()
     x_first(1).wait_recv()
     summed(1)
     send(ring2("b2", 1), r.b2_out, 1, r.bsum[1, part_rows:])
+    give(1)
     x_first(2).wait_recv()
     summed(2)
     send(ring2("b2", 2), r.b2_out, 2, r.bsum[2, :part_rows])
-    give(1)
     mixes = [one_way("mx", c, partner) for c in range(2)]
     mix(2, r.mx_out, 0)
     mixes[0].start()
-    back[1].middle()
     ring1("b1", 0).wait_recv()
     send(ring2("b2", 0), r.b2_out, 0, r.bsum[1, :part_rows] + r.b1_in[0].astype(F32))
     ring1("b1", 1).wait_recv()
     send(ring2("b2", 3), r.b2_out, 3, r.bsum[2, part_rows:] + r.b1_in[1].astype(F32))
-    back[2].middle()
-    mix(3, r.mx_out, 1)
-    mixes[1].start()
     for slot in range(4):
         ring2("a2", slot).wait_recv()
     for s in range(2):
@@ -398,7 +393,10 @@
     r.ax_out[...] = r.total[1 - xl].astype(BF16)
     x_last = remote(r.ax_out, r.ax_in, r.ax_ss.at[0], r.ax_rs.at[0], x_device)
     x_last.start()
+    back[2].middle()
     back[3].middle()
+    mix(3, r.mx_out, 1)
+    mixes[1].start()
     x_first(3).wait_recv()
     summed(3)
     for slot in range(4):
@@ -412,10 +410,17 @@
     x_last.wait_recv()
     r.s0_out[...] = (r.total[xl] + r.ax_in[...].astype(F32)).astype(BF16).reshape(r.s0_out.shape)
     over_z[0].start()
+    back[0].middle()
+    back[1].middle()
     mix(1, r.mx_own, 1)
 
     r.rows[0, :, halves[0]] = back[0].finish()
     r.rows[0, :, halves[1]] = back[1].finish()
+    for b in (1, 0):
+        over_z[b].wait_recv()
+        r.last_out[:, blocks[b]] = jnp.sum((r.s0_in, r.s1_in)[b][...].astype(F32), axis=0)
+    last = remote(r.last_out, r.last_in, r.last_sem.at[0], r.last_sem.at[1], sibling)
+    last.start()
     for c in range(2):
         mixes[c].wait_recv()
     mixed_rows = []
@@ -424,11 +429,6 @@
         frames = jnp.where(slots[:, :1] < 0.5 * ABSENT, slots, 0.0)
         mixed_rows.append((frames + 0.5 * (r.mx_own[c].astype(F32) + r.mx_in[c].astype(F32))).astype(BF16))
     r.mixed[...] = swap_rows(2, ndp, jnp.concatenate(mixed_rows, axis=0))
-    for b in (1, 0):
-        over_z[b].wait_recv()
-        r.last_out[:, blocks[b]] = jnp.sum((r.s0_in, r.s1_in)[b][...].astype(F32), axis=0)
-    last = remote(r.last_out, r.last_in, r.last_sem.at[0], r.last_sem.at[1], sibling)
-    last.start()
     r.rows[1, :, halves[0]] = back[2].finish()
     r.rows[1, :, halves[1]] = back[3].finish()
     r.grad_source[...] = (t_dot(r.hot[:ndp], r.rows[0]) + t_dot(r.hot[ndp:], r.rows[1])).astype(BF16)

time: 106 us -> 102 us (0.962)
  Pallas kernels: 105 us -> 100 us
    pallas_call x1, Pallas kernels: 102 us -> 98.1 us  [local(): pl.pallas_call(functools.partial(kernel, ndp, list(inputs) + list(outputs...]
where the time goes in v5:
time: 102 us
  Pallas kernels  100 us (98%)
  between operations  1.29 us (1%)
    pallas_call x1, Pallas kernels, local(): pl.pallas_call(functools.partial(kernel, ndp, list(inputs) + list(outputs...  98.1 us
    pallas_call x1, Pallas kernels, local(): pl.pallas_call(finish_kernel, out_shape=list(outputs.values()), in_specs=...  2.31 us

profile of v5, /device:TPU:1, one launch (start us, length us, event | category | flops | bytes accessed | tf_op | source)
XLA Modules:
  0.0 101.7 jit_solution(2927422899911017227)
XLA Ops:
  1.3 98.1 %module.1 = (bf16[256,1536]{1,0:T(8,128)(2,1)}, bf16[128,1536]{1,0:T(8,128)(2,1)}, f32[12,1536]{1,0:T(8,128)}) custom-call(bf16[128,1536]{1,0:T(8,128)(2,1)} %refs_0_.1, s32[1,128]{1,0:T(1,128)} %bitcast.4, s32[1,1]{1,0:T(1,128)} %bitcast.3.refs_2_, f32[1536]{0:T(1024)} %refs_3_.1, bf16[256,1536]{1,0:T(8,128)(2,1)} %refs_4_.1, bf16[1536,1536]{1,0:T(8,128)(2,1)} %refs_5_.1, ...), custom_call_target="tpu_custom_call" | custom-call | tf_op jit(solution)/shard_map/module/pallas_call | solution.py:540
  99.3 2.3 %finish.1 = (bf16[256,1536]{1,0:T(8,128)(2,1)}, bf16[128,1536]{1,0:T(8,128)(2,1)}, f32[12,1536]{1,0:T(8,128)}) custom-call(bf16[256,1536]{1,0:T(8,128)(2,1)} %get-tuple-element.9.mixed, bf16[128,1536]{1,0:T(8,128)(2,1)} %get-tuple-element.10.grad_source, f32[12,1536]{1,0:T(8,128)} %get-tuple-element.11.grad_out), custom_call_target="tpu_custom_call" | custom-call | tf_op jit(solution)/shard_map/finish/pallas_call | solution.py:551

commit v6 on v5

--- a/solution.py
+++ b/solution.py
@@ -180,12 +180,12 @@
 
     there = [routed("a" + str(i), i < 2) for i in range(4)]
     leaving = outgoing(0)
+    load_cot.wait()
+    cot_copy = remote(r.cot, r.cot_in, r.cot_sem.at[0], r.cot_sem.at[1], partner)
     pl.semaphore_wait(barrier, nz + GROUP - 1)
+    cot_copy.start()
     there[0].start(leaving[:, halves[0]])
     there[1].start(leaving[:, halves[1]])
-    load_cot.wait()
-    cot_copy = remote(r.cot, r.cot_in, r.cot_sem.at[0], r.cot_sem.at[1], partner)
-    cot_copy.start()
     leaving = outgoing(1)
     there[2].start(leaving[:, halves[0]])
     there[3].start(leaving[:, halves[1]])
@@ -267,26 +267,22 @@
     order_cot(1, r.cot_in[...])
     land(2)
     land(3)
-    mix(0, r.mx_own, 0)
+    process(1)
     frames_over[0].wait_recv()
     frames_over[1].wait_recv()
     process(2)
     sums = [one_way("gs", i // 2, partner, i % 2) for i in range(4)]
-
-    def send_sums(c):
-        for part in range(2):
-            scaled_grad(2 + c, r.gs_out, c, part * wide, wide)
-            sums[2 * c + part].start()
-
-    send_sums(0)
-    process(1)
+    scaled_grad(2, r.gs_out, 0)
     scaled_grad(1, r.gs_own, 1)
-    for route in there:
-        route.wait_send()
+    mix(0, r.mx_own, 0)
     frames_over[2].wait_recv()
     frames_over[3].wait_recv()
+    sums[0].start()
+    sums[1].start()
     process(3)
-    send_sums(1)
+    for part in range(2):
+        scaled_grad(3, r.gs_out, 1, part * wide, wide)
+        sums[2 + part].start()
 
     up, down, opposite = lax.rem(y + 1, RING), lax.rem(y + 3, RING), lax.rem(y + 2, RING)
     order = [opposite, up, down, y]
@@ -413,6 +409,18 @@
     back[0].middle()
     back[1].middle()
     mix(1, r.mx_own, 1)
+    x_last.wait_send()
+    cot_copy.wait_send()
+    for copy in sums + frames_over + there:
+        copy.wait_send()
+    for name in ("a", "b"):
+        for slot in range(2):
+            ring1(name + "1", slot).wait_send()
+        for slot in range(4):
+            ring2(name + "2", slot).wait_send()
+    for i in range(4):
+        to_sibling(i).wait_send()
+        x_first(i).wait_send()
 
     r.rows[0, :, halves[0]] = back[0].finish()
     r.rows[0, :, halves[1]] = back[1].finish()
@@ -443,18 +451,8 @@
     r.grad_out[:, half:] = jnp.where(is_low, other, own)
 
     last.wait_send()
-    cot_copy.wait_send()
-    x_last.wait_send()
-    for copy in sums + mixes + frames_over + back + over_z:
+    for copy in mixes + back + over_z:
         copy.wait_send()
-    for name in ("a", "b"):
-        for slot in range(2):
-            ring1(name + "1", slot).wait_send()
-        for slot in range(4):
-            ring2(name + "2", slot).wait_send()
-    for i in range(4):
-        to_sibling(i).wait_send()
-        x_first(i).wait_send()
 
 
 def finish_kernel(mixed, grad_source, grad_out, mixed_out, grad_source_out, grad_out_out):

time: 102 us -> 99.5 us (0.975)
  Pallas kernels: 100 us -> 98.1 us
    pallas_call x1, Pallas kernels: 98.1 us -> 95.8 us  [local(): pl.pallas_call(functools.partial(kernel, ndp, list(inputs) + list(outputs...]
where the time goes in v6:
time: 99.5 us; the launch traced here: 99.4 us
  Pallas kernels  98.1 us (99%)
  between operations  1.29 us (1%)
    pallas_call x1, Pallas kernels, local(): pl.pallas_call(functools.partial(kernel, ndp, list(inputs) + list(outputs...  95.8 us
    pallas_call x1, Pallas kernels, local(): pl.pallas_call(finish_kernel, out_shape=list(outputs.values()), in_specs=...  2.31 us

profile of v6, /device:TPU:1, one launch (start us, length us, event | category | flops | bytes accessed | tf_op | source)
XLA Modules:
  0.0 99.4 jit_solution(3563610766708196571)
XLA Ops:
  1.3 95.8 %module.1 = (bf16[256,1536]{1,0:T(8,128)(2,1)}, bf16[128,1536]{1,0:T(8,128)(2,1)}, f32[12,1536]{1,0:T(8,128)}) custom-call(bf16[128,1536]{1,0:T(8,128)(2,1)} %refs_0_.1, s32[1,128]{1,0:T(1,128)} %bitcast.4, s32[1,1]{1,0:T(1,128)} %bitcast.3.refs_2_, f32[1536]{0:T(1024)} %refs_3_.1, bf16[256,1536]{1,0:T(8,128)(2,1)} %refs_4_.1, bf16[1536,1536]{1,0:T(8,128)(2,1)} %refs_5_.1, ...), custom_call_target="tpu_custom_call" | custom-call | tf_op jit(solution)/shard_map/module/pallas_call | solution.py:538
  97.1 2.3 %finish.1 = (bf16[256,1536]{1,0:T(8,128)(2,1)}, bf16[128,1536]{1,0:T(8,128)(2,1)}, f32[12,1536]{1,0:T(8,128)}) custom-call(bf16[256,1536]{1,0:T(8,128)(2,1)} %get-tuple-element.9.mixed, bf16[128,1536]{1,0:T(8,128)(2,1)} %get-tuple-element.10.grad_source, f32[12,1536]{1,0:T(8,128)} %get-tuple-element.11.grad_out), custom_call_target="tpu_custom_call" | custom-call | tf_op jit(solution)/shard_map/finish/pallas_call | solution.py:549

commit v7 on v6

--- a/solution.py
+++ b/solution.py
@@ -235,13 +235,13 @@
             r.act[rows, n] = jnp.where(present, hidden * gate, 0.0).astype(BF16)
             r.gh[rows, n] = (grad_act * gate * (1.0 + hidden * (1.0 - gate))).astype(BF16)
 
-        tiles(units, 512, tile)
+        tiles(units, 768, tile)
 
     def scaled_grad(k, out, c, start=0, length=None):
         def tile(n):
             out[c, :, n] = dot_t(r.gh[pl.ds(k * ndp, ndp), :], r.win[n, :]).astype(BF16)
 
-        tiles(length or width, 384, tile, start)
+        tiles(length or width, 768, tile, start)
 
     def mix(k, out, c):
         def tile(n):
@@ -249,7 +249,7 @@
                 r.act[pl.ds(k * ndp, ndp), :], r.wout[:, n], preferred_element_type=F32
             ).astype(BF16)
 
-        tiles(width, 512, tile)
+        tiles(width, 768, tile)
 
     frames_over = [one_way("fr", i // 2, partner, i % 2) for i in range(4)]
 
@@ -280,9 +280,6 @@
     sums[0].start()
     sums[1].start()
     process(3)
-    for part in range(2):
-        scaled_grad(3, r.gs_out, 1, part * wide, wide)
-        sums[2 + part].start()
 
     up, down, opposite = lax.rem(y + 1, RING), lax.rem(y + 3, RING), lax.rem(y + 2, RING)
     order = [opposite, up, down, y]
@@ -299,6 +296,9 @@
     for i in range(4):
         r.sib_out[pl.ds(2 * order[i], 2)] = product(order[i], 1 - core).astype(BF16)
         to_sibling(i).start()
+    for part in range(2):
+        scaled_grad(3, r.gs_out, 1, part * wide, wide)
+        sums[2 + part].start()
 
     def keep(i):
         r.mine[pl.ds(2 * order[i], 2)] = product(order[i], core)

time: 99.5 us -> 99.2 us (level)
  no operation moved by 1% of the time
where the time goes in v7:
time: 99.2 us; the launch traced here: 99.1 us
  Pallas kernels  97.8 us (99%)
  between operations  1.29 us (1%)
    pallas_call x1, Pallas kernels, local(): pl.pallas_call(functools.partial(kernel, ndp, list(inputs) + list(outputs...  95.5 us
    pallas_call x1, Pallas kernels, local(): pl.pallas_call(finish_kernel, out_shape=list(outputs.values()), in_specs=...  2.31 us

profile of v7, /device:TPU:1, one launch (start us, length us, event | category | flops | bytes accessed | tf_op | source)
XLA Modules:
  0.0 99.1 jit_solution(10344846142481001178)
XLA Ops:
  1.3 95.5 %module.1 = (bf16[256,1536]{1,0:T(8,128)(2,1)}, bf16[128,1536]{1,0:T(8,128)(2,1)}, f32[12,1536]{1,0:T(8,128)}) custom-call(bf16[128,1536]{1,0:T(8,128)(2,1)} %refs_0_.1, s32[1,128]{1,0:T(1,128)} %bitcast.4, s32[1,1]{1,0:T(1,128)} %bitcast.3.refs_2_, f32[1536]{0:T(1024)} %refs_3_.1, bf16[256,1536]{1,0:T(8,128)(2,1)} %refs_4_.1, bf16[1536,1536]{1,0:T(8,128)(2,1)} %refs_5_.1, ...), custom_call_target="tpu_custom_call" | custom-call | tf_op jit(solution)/shard_map/module/pallas_call | solution.py:538
  96.8 2.3 %finish.1 = (bf16[256,1536]{1,0:T(8,128)(2,1)}, bf16[128,1536]{1,0:T(8,128)(2,1)}, f32[12,1536]{1,0:T(8,128)}) custom-call(bf16[256,1536]{1,0:T(8,128)(2,1)} %get-tuple-element.9.mixed, bf16[128,1536]{1,0:T(8,128)(2,1)} %get-tuple-element.10.grad_source, f32[12,1536]{1,0:T(8,128)} %get-tuple-element.11.grad_out), custom_call_target="tpu_custom_call" | custom-call | tf_op jit(solution)/shard_map/finish/pallas_call | solution.py:549

commit v8 on v7

--- a/solution.py
+++ b/solution.py
@@ -389,10 +389,6 @@
     r.ax_out[...] = r.total[1 - xl].astype(BF16)
     x_last = remote(r.ax_out, r.ax_in, r.ax_ss.at[0], r.ax_rs.at[0], x_device)
     x_last.start()
-    back[2].middle()
-    back[3].middle()
-    mix(3, r.mx_out, 1)
-    mixes[1].start()
     x_first(3).wait_recv()
     summed(3)
     for slot in range(4):
@@ -403,6 +399,10 @@
         r.bsum[3, at] = r.bsum[3, at] + r.b2_in[s].astype(F32) + r.b2_in[2 + s].astype(F32)
     r.s1_out[...] = r.bsum[3].astype(BF16).reshape(r.s1_out.shape)
     over_z[1].start()
+    back[2].middle()
+    back[3].middle()
+    mix(3, r.mx_out, 1)
+    mixes[1].start()
     x_last.wait_recv()
     r.s0_out[...] = (r.total[xl] + r.ax_in[...].astype(F32)).astype(BF16).reshape(r.s0_out.shape)
     over_z[0].start()

time: 99.2 us -> 99.7 us (level)
  no operation moved by 1% of the time
where the time goes in v8:
time: 99.7 us; the launch traced here: 99.6 us
  Pallas kernels  98.3 us (99%)
  between operations  1.29 us (1%)
    pallas_call x1, Pallas kernels, local(): pl.pallas_call(functools.partial(kernel, ndp, list(inputs) + list(outputs...  96 us
    pallas_call x1, Pallas kernels, local(): pl.pallas_call(finish_kernel, out_shape=list(outputs.values()), in_specs=...  2.31 us

profile of v8, /device:TPU:1, one launch (start us, length us, event | category | flops | bytes accessed | tf_op | source)
XLA Modules:
  0.0 99.6 jit_solution(2172510104571582145)
XLA Ops:
  1.3 96.0 %module.1 = (bf16[256,1536]{1,0:T(8,128)(2,1)}, bf16[128,1536]{1,0:T(8,128)(2,1)}, f32[12,1536]{1,0:T(8,128)}) custom-call(bf16[128,1536]{1,0:T(8,128)(2,1)} %refs_0_.1, s32[1,128]{1,0:T(1,128)} %bitcast.4, s32[1,1]{1,0:T(1,128)} %bitcast.3.refs_2_, f32[1536]{0:T(1024)} %refs_3_.1, bf16[256,1536]{1,0:T(8,128)(2,1)} %refs_4_.1, bf16[1536,1536]{1,0:T(8,128)(2,1)} %refs_5_.1, ...), custom_call_target="tpu_custom_call" | custom-call | tf_op jit(solution)/shard_map/module/pallas_call | solution.py:538
  97.3 2.3 %finish.1 = (bf16[256,1536]{1,0:T(8,128)(2,1)}, bf16[128,1536]{1,0:T(8,128)(2,1)}, f32[12,1536]{1,0:T(8,128)}) custom-call(bf16[256,1536]{1,0:T(8,128)(2,1)} %get-tuple-element.9.mixed, bf16[128,1536]{1,0:T(8,128)(2,1)} %get-tuple-element.10.grad_source, f32[12,1536]{1,0:T(8,128)} %get-tuple-element.11.grad_out), custom_call_target="tpu_custom_call" | custom-call | tf_op jit(solution)/shard_map/finish/pallas_call | solution.py:549
